TPU v7x, 32 devices: a whole 2x2x4 slice. The times are simulated.
32 devices in a mesh: sky: 2 (over x), tm: 16 (over z, y, core).
Axes of the slice: x: 2, y: 2, z: 4, core: 2. Of those that a mesh axis runs over, the one named last changes fastest.
Arguments:
- series: bfloat16 [4, 4, 1024, 2048], P('sky', None, 'tm'), parts along dimension 0, may hold values from -6 to 6
- antenna: float32 [4, 3], P('sky'), parts along dimension 0, as said below
- offsets: int32 [16, 2], P('sky'), parts along dimension 0, may hold values from -8 to 8, as said below
Outputs:
- detection: float32 [16, 1024, 2048], P('sky', 'tm'), parts along dimension 0
There are 2 independent parts, one for each index of `sky`. A program takes and returns all parts, laid end to end along the dimension named above; each array names one. Nothing has to cross between parts.
Inputs may be any that keep to these rules, and one draw needn't show every extreme that they name: `offsets`: both -8 and 8 occur in every draw. `antenna`: A and B are positive and C C is at most 0.49 A B in every row.
All inputs are finite; a program needn't handle non-finite values.
Results may differ from a plain program's by a relative error of at most 0.0032.
Values may be sent and summed in bfloat16 or wider, within the bound.
No kernel may reach another device: no remote copies, remote signals or barrier semaphores. Data moves between devices by JAX's collectives and lax.ppermute only.
A program may use at most 128 MiB of HBM per device.

v0:
```python
import functools
import math

import jax
import jax.numpy as jnp
import numpy as np
from jax import lax
from jax.experimental import pallas as pl
from jax.experimental.pallas import tpu as pltpu
from jax.sharding import PartitionSpec as P

DMAX = 8
LANES = 128
BF16 = jnp.bfloat16
F32 = jnp.float32
SEG, LOWEST, TOP, FIRST, LAST = range(5)
SMEM = pl.BlockSpec(memory_space=pltpu.SMEM)
VMEM = pl.BlockSpec(memory_space=pltpu.VMEM)
ANY = pl.BlockSpec(memory_space=pl.ANY)


def params(mebibytes):
    return pltpu.CompilerParams(vmem_limit_bytes=mebibytes * 1024 * 1024)


def cost(flops, moved):
    return pl.CostEstimate(flops=flops, bytes_accessed=moved, transcendentals=0)


def dft_table(rows, cols, length):
    products = rows[:, None].astype(np.int64) * cols[None, :] % length
    angle = products.astype(np.float32) * np.float32(2.0 * math.pi / length)
    return np.cos(angle), -np.sin(angle)


def in_hbm(x):
    return pltpu.with_memory_space_constraint(x, pltpu.HBM)


def dot(x, y):
    return jnp.dot(x, y, preferred_element_type=F32)


def pack_kernel(x_ref, out_ref):
    cols = out_ref.shape[-1]
    for piece in range(out_ref.shape[0]):
        out_ref[piece] = x_ref[0, :, :, piece * cols : (piece + 1) * cols]


def pack(series, groups):
    segs, comps, rows, width = series.shape
    shape = (segs * groups, comps, rows, width // groups)
    return pl.pallas_call(
        pack_kernel,
        grid=(segs,),
        in_specs=[pl.BlockSpec((1, comps, rows, width), lambda s: (s, 0, 0, 0))],
        out_specs=pl.BlockSpec((groups,) + shape[1:], lambda s: (s, 0, 0, 0)),
        out_shape=pltpu.HBM(shape, BF16),
        compiler_params=params(16),
        cost_estimate=cost(0, 4 * math.prod(shape)),
        name="pack",
    )(in_hbm(series))


def first_kernel(half_ref, x_ref, sort_ref, w_ref, br_ref, bi_ref, vr_ref, vi_ref, *refs):
    out_ref, sorted_ref = refs[-2:]
    tile, length = w_ref.shape[1] // 2, w_ref.shape[2]
    comps, cols = x_ref.shape[1], x_ref.shape[-1]
    spots = [slice(comp * cols, (comp + 1) * cols) for comp in range(comps)]

    @pl.when(pl.program_id(0) == 0)
    def _():
        for comp, spot in enumerate(spots):
            sorted_ref[:, spot] = dot(x_ref[:, comp].reshape(length, cols), sort_ref[...]).astype(BF16)

    shape = (out_ref.shape[0],) + out_ref.shape[2:]
    by_real, by_imag = vr_ref[...], vi_ref[...]
    t_real = br_ref[...] * by_real - bi_ref[...] * by_imag
    t_imag = br_ref[...] * by_imag + bi_ref[...] * by_real
    both = dot(w_ref[0], sorted_ref[...])
    with_real, with_imag = both[:tile], both[tile:]
    for lead in range(0, comps, 2):
        real_part = with_real[:, spots[lead]] - with_imag[:, spots[lead + 1]]
        imag_part = with_imag[:, spots[lead]] + with_real[:, spots[lead + 1]]
        out_ref[:, lead] = (real_part * t_real - imag_part * t_imag).astype(BF16).reshape(shape)
        out_ref[:, lead + 1] = (real_part * t_imag + imag_part * t_real).astype(BF16).reshape(shape)


def first_pass(pieces, half, order, table, bases, turns, groups, after):
    count, comps, rows, cols = pieces.shape
    length = count * rows
    per_half = groups * rows
    tile = table.shape[1] // 2
    steps = per_half // tile
    sort = np.zeros((cols, cols), np.float32)
    sort[order, np.arange(cols)] = 1.0
    strip = lambda width: pl.BlockSpec((tile, width), lambda t, half: (half[0] * steps + t, 0))
    return pl.pallas_call(
        first_kernel,
        grid_spec=pltpu.PrefetchScalarGridSpec(
            num_scalar_prefetch=1,
            grid=(steps,),
            in_specs=[VMEM, pl.BlockSpec((cols, cols), lambda t, half: (0, 0))]
            + [pl.BlockSpec((1,) + table.shape[1:], lambda t, half: (half[0] * steps + t, 0, 0))]
            + [strip(cols)] * 2
            + [strip(1)] * 2
            + [ANY] * len(after),
            out_specs=pl.BlockSpec((tile // rows, comps, rows, cols), lambda t, half: (t, 0, 0, 0)),
            scratch_shapes=[pltpu.VMEM((length, comps * cols), BF16)],
        ),
        out_shape=pltpu.HBM((groups, comps, rows, cols), BF16),
        compiler_params=params(24),
        cost_estimate=cost(4 * comps * per_half * length * cols, 4 * per_half * length),
        name="first_pass",
    )(half, pieces, in_hbm(sort.astype(BF16)), in_hbm(table), *map(in_hbm, bases), *turns, *after)


def fstat_kernel(length, place_ref, coef_ref, z_ref, w_ref, *refs):
    fstat_ref, tail_ref, head_ref, lhs_ref = refs[-4:]
    step = pl.program_id(0)

    @pl.when(step == 0)
    def _():
        groups, cols = z_ref.shape[0], z_ref.shape[-1] // 2
        for source in range(groups):
            piece = z_ref[source].reshape(lhs_ref.shape[1], 2 * cols)
            for parity in range(2):
                at = slice(source * cols, (source + 1) * cols)
                lhs_ref[parity, :, at] = piece[:, parity * cols : (parity + 1) * cols]

    rows, width = fstat_ref.shape
    tile = w_ref.shape[-1]
    even, odd = lhs_ref[0], lhs_ref[1]
    even_real, even_imag = dot(even, w_ref[0, 0]), dot(even, w_ref[0, 1])
    odd_real, odd_imag = dot(odd, w_ref[0, 2]), dot(odd, w_ref[0, 3])
    coef_a, coef_b, coef_c = [jnp.full((1, tile), coef_ref[place_ref[SEG], at], F32) for at in range(3)]
    scale = 1.0 / ((coef_a * coef_b - coef_c * coef_c) * length)
    coef_a, coef_b, coef_c = coef_a * scale, coef_b * scale, 2.0 * coef_c * scale
    tails, heads = [], []
    for half in range(2):
        by_real = even_real - odd_real if half else even_real + odd_real
        by_imag = even_imag - odd_imag if half else even_imag + odd_imag
        part = lambda x, comp: x[comp * rows : (comp + 1) * rows]
        a_real = part(by_real, 0) - part(by_imag, 1)
        a_imag = part(by_imag, 0) + part(by_real, 1)
        b_real = part(by_real, 2) - part(by_imag, 3)
        b_imag = part(by_imag, 2) + part(by_real, 3)
        fstat = (
            coef_b * (a_real * a_real + a_imag * a_imag)
            + coef_a * (b_real * b_real + b_imag * b_imag)
            - coef_c * (a_real * b_real + a_imag * b_imag)
        )
        tails.append(fstat[rows - DMAX :])
        heads.append(fstat[:DMAX])
        at = pl.ds(pl.multiple_of(half * (width // 2) + step * tile, tile), tile)
        fstat_ref[:, at] = fstat.astype(fstat_ref.dtype)
    at = pl.ds(pl.multiple_of(step * tile, tile), tile)
    tail_ref[:, at] = jnp.concatenate(tails, axis=0).astype(tail_ref.dtype)
    head_ref[:, at] = jnp.concatenate(heads, axis=0).astype(head_ref.dtype)


def fstat_pass(z, place, table, antenna, length, kind, after=()):
    groups, comps, rows, cols = z.shape
    width = groups * cols
    rim = (2 * DMAX, width // 2)
    still = lambda shape: pl.BlockSpec(shape, lambda t: (0, 0))
    return pl.pallas_call(
        functools.partial(fstat_kernel, length),
        grid=(table.shape[0],),
        in_specs=[SMEM, SMEM, VMEM, pl.BlockSpec((1,) + table.shape[1:], lambda t: (t, 0, 0, 0))] + [ANY] * len(after),
        out_specs=[still((rows, width)), still(rim), still(rim)],
        out_shape=[jax.ShapeDtypeStruct((rows, width), kind)] + [jax.ShapeDtypeStruct(rim, kind)] * 2,
        scratch_shapes=[pltpu.VMEM((2, comps * rows, width // 2), BF16)],
        compiler_params=params(24),
        cost_estimate=cost(2 * comps * rows * width * width, 2 * width * width),
        name="fstat_pass",
    )(place, antenna, z, in_hbm(table), *after)


def gate(x, after):
    return pl.pallas_call(
        lambda *refs: None,
        in_specs=[ANY, ANY],
        out_specs=ANY,
        out_shape=pltpu.HBM(x.shape, x.dtype),
        input_output_aliases={0: 0},
        compiler_params=params(2),
        cost_estimate=cost(0, 0),
        name="gate",
    )(in_hbm(x), after)


def detect_kernel(offsets_ref, place_ref, other_ref, own_ref, *refs):
    early_refs, late_refs, out_ref, wide_refs = refs[:2], refs[2:4], refs[4], refs[5:]
    rows = own_ref.shape[0]

    @pl.when(pl.program_id(0) == 0)
    def _():
        is_first, is_last, seg = place_ref[FIRST] == 1, place_ref[LAST] == 1, place_ref[SEG]
        lowest, top = place_ref[LOWEST] == 1, place_ref[TOP] == 1
        width = own_ref.shape[1]
        unfold = lambda ref: jnp.concatenate([ref[...].astype(F32)[:DMAX], ref[...].astype(F32)[DMAX:]], axis=1)
        early, late = [unfold(ref) for ref in early_refs], [unfold(ref) for ref in late_refs]

        def widen(wide_ref, middle, lower, upper):
            lower = jnp.where(is_first, pltpu.roll(lower, 1, 1), lower)
            upper = jnp.where(is_last, pltpu.roll(upper, width - 1, 1), upper)
            for strip in range(width // LANES):
                at = slice(strip * LANES, (strip + 1) * LANES)
                wide_ref[strip, :DMAX] = lower[:, at]
                wide_ref[strip, DMAX : DMAX + rows] = middle[:, at]
                wide_ref[strip, DMAX + rows :] = upper[:, at]

        def place(own_wide, other_wide):
            lower = jnp.where(lowest, early[0], late[0]), jnp.where(lowest, late[0], early[0])
            upper = jnp.where(top, early[1], late[1]), jnp.where(top, late[1], early[1])
            widen(own_wide, own_ref[...], lower[0], upper[0])
            widen(other_wide, other_ref[...].astype(F32), lower[1], upper[1])

        @pl.when(seg == 0)
        def _():
            place(wide_refs[0], wide_refs[1])

        @pl.when(seg != 0)
        def _():
            place(wide_refs[1], wide_refs[0])

    for at in range(out_ref.shape[0]):
        template = pl.program_id(0) * out_ref.shape[0] + at
        begins = [DMAX + offsets_ref[template, s] for s in range(len(wide_refs))]
        for strip in range(own_ref.shape[1] // LANES):
            total = wide_refs[0][strip, pl.ds(begins[0], rows), :]
            for begin, wide_ref in zip(begins[1:], wide_refs[1:]):
                total = total + wide_ref[strip, pl.ds(begin, rows), :]
            out_ref[at, :, strip * LANES : (strip + 1) * LANES] = total * (1.0 / len(wide_refs))


def detect(offsets, place, other, own, early, late):
    templates = offsets.shape[0]
    rows, width = own.shape
    batch = 2 - templates % 2
    return pl.pallas_call(
        detect_kernel,
        grid=(templates // batch,),
        in_specs=[SMEM, SMEM] + [VMEM] * 6,
        out_specs=pl.BlockSpec((batch, rows, width), lambda t: (t, 0, 0)),
        out_shape=jax.ShapeDtypeStruct((templates, rows, width), F32),
        scratch_shapes=[pltpu.VMEM((width // LANES, rows + 2 * DMAX, LANES), F32)] * 2,
        compiler_params=params(8),
        cost_estimate=cost(3 * templates * rows * width, 4 * templates * rows * width),
        name="detect",
    )(offsets, place, other, own, *early, *late)


def local(series, antenna, offsets):
    devices = lax.axis_size("tm")
    index = lax.axis_index("tm")
    segs, _, rows, width = series.shape
    slow = devices * rows
    length = slow * width
    groups = devices // segs
    cols = width // groups
    seg, member = index // groups, index % groups
    place = jnp.stack([seg, member == 0, member == groups - 1, index == 0, index == devices - 1]).astype(jnp.int32)

    bins = np.arange(slow)
    tile = min(256, groups * rows)
    short = np.stack(dft_table(bins, bins, slow)).astype(BF16).reshape(2, -1, tile, slow)
    short = short.transpose(1, 0, 2, 3).reshape(-1, 2 * tile, slow)
    fast = np.arange(width // 2)
    tile = min(256, width // 2)
    long = np.stack([x.astype(BF16) for parity in range(2) for x in dft_table(2 * fast + parity, fast, width)])
    long = long.reshape(4, width // 2, -1, tile).transpose(2, 0, 1, 3)
    order = np.concatenate([np.arange(0, cols, 2), np.arange(1, cols, 2)])
    bases = dft_table(bins, order, length)
    angle = (jnp.arange(slow, dtype=jnp.int32) * (member * cols) % length).astype(F32) * (2.0 * math.pi / length)
    turns = (jnp.cos(angle)[:, None], -jnp.sin(angle)[:, None])

    halves = [[g * groups + i for i in range(groups)] for g in range(segs)]
    trade = functools.partial(lax.all_to_all, axis_name="tm", split_axis=0, concat_axis=0, tiled=True)
    pieces = trade(pack(series, groups))

    def turn(half, *after):
        return first_pass(pieces, half[None], order, short, bases, turns, groups, after)

    def move(x, by):
        return lax.ppermute(x, "tm", [(i, (i + by) % devices) for i in range(devices)])

    far = turn(1 - seg)
    near = turn(seg, far)
    far = trade(far, axis_index_groups=halves)
    near = trade(gate(near, far), axis_index_groups=halves)
    far, far_tail, far_head = fstat_pass(far, place, long, antenna, length, BF16)
    other = move(far, groups)
    own, tail, head = fstat_pass(near, place, long, antenna, length, F32, (far,))
    early = [move(far_tail, groups + 1), move(far_head, groups - 1)]
    late = [move(tail, 1), move(head, -1)]
    return detect(offsets, place, other, own, early, late)


def solution(mesh):
    return jax.shard_map(
        local,
        mesh=mesh,
        in_specs=(P("sky", None, "tm", None), P("sky", None), P("sky", None)),
        out_specs=P("sky", "tm", None),
        check_vma=False,
    )
```

profile of v0, /device:TPU:0, one launch (start us, length us, event | category | flops | bytes accessed | tf_op | source)
XLA Modules:
  0.0 123.6 jit_solution(718521078572333475)
XLA Ops:
  0.0 2.6 %pack.1 = bf16[16,4,64,256]{3,2,1,0:T(8,128)(2,1)} custom-call(bf16[2,4,64,2048]{3,2,1,0:T(8,128)(2,1)} %x_ref.1), custom_call_target="tpu_custom_call" | custom-call | bytes 4194304 | tf_op jit(solution)/shard_map/pack/pallas_call | solution.py:53
  2.6 7.4 %all-to-all-start = ((bf16[16,4,64,256]{3,2,1,0:T(8,128)(2,1)}), bf16[16,4,64,256]{3,2,1,0:T(8,128)(2,1)S(1)}, u32[]{:S(2)}, u32[]{:S(2)}) async-start(bf16[16,4,64,256]{3,2,1,0:T(8,128)(2,1)} %pack.1), calls=%async_computation | async-start | bytes 4194304 | tf_op jit(solution)/shard_map/all_to_all | solution.py:281
  10.1 1.0 copy.12
  11.1 2.8 %sine_negate_fusion = (f32[1024,1]{1,0:T(8,128)S(1)}, f32[1024,1]{1,0:T(8,128)S(1)}) fusion(f32[1024,1]{1,0:T(8,128)} %copy.12), kind=kLoop, calls=%fused_computation | loop fusion | flops 2048 | bytes 12288 | tf_op jit(solution)/shard_map/neg | solution.py:277
  13.9 0.0 copy-start.1
  13.9 37.2 %all-to-all-done.x_ref = bf16[16,4,64,256]{3,2,1,0:T(8,128)(2,1)S(1)} async-done(((bf16[16,4,64,256]{3,2,1,0:T(8,128)(2,1)}), bf16[16,4,64,256]{3,2,1,0:T(8,128)(2,1)S(1)}, u32[]{:S(2)}, u32[]{:S(2)}) %all-to-all-start) | async-done | bytes 2097184 | tf_op jit(solution)/shard_map/all_to_all | solution.py:281
  51.1 5.7 %first_pass.2.refs_0_ = bf16[8,4,64,256]{3,2,1,0:T(8,128)(2,1)} custom-call(s32[1]{0:T(128)} %bitcast.5.half_ref, bf16[16,4,64,256]{3,2,1,0:T(8,128)(2,1)S(1)} %all-to-all-done.x_ref, bf16[256,256]{1,0:T(8,128)(2,1)} %constant.63.clone.sort_ref, bf16[4,512,1024]{2,1,0:T(8,128)(2,1)} %constant.64.clone.w_ref, f32[1024,256]{1,0:T(8,128)} %constant.65.clone.br_ref, ...), custom_call_target="tpu_custom_call" | custom-call | flops 2147483648 | bytes 2097152 | tf_op jit(solution)/shard_map/first_pass/pallas_call | solution.py:98
  56.8 10.3 %all-to-all-start.1 = ((bf16[8,4,64,256]{3,2,1,0:T(8,128)(2,1)}), bf16[8,4,64,256]{3,2,1,0:T(8,128)(2,1)S(1)}, u32[]{:S(2)}, u32[]{:S(2)}) async-start(bf16[8,4,64,256]{3,2,1,0:T(8,128)(2,1)} %first_pass.2.refs_0_), calls=%async_computation.1 | async-start | bytes 2097152 | tf_op jit(solution)/shard_map/all_to_all | solution.py:291
  67.1 1.3 %copy-done = bf16[8,4,64,256]{3,2,1,0:T(8,128)(2,1)S(1)} copy-done((bf16[8,4,64,256]{3,2,1,0:T(8,128)(2,1)S(1)}, bf16[8,4,64,256]{3,2,1,0:T(8,128)(2,1)}, u32[]{:S(2)}) %copy-start) | copy-done | bytes 1048600
  68.4 1.0 copy-done.2
  69.4 1.0 copy-done.4
  70.4 5.7 %first_pass.3.refs_0_ = bf16[8,4,64,256]{3,2,1,0:T(8,128)(2,1)} custom-call(s32[1]{0:T(128)} %bitcast.half_ref, bf16[16,4,64,256]{3,2,1,0:T(8,128)(2,1)S(1)} %all-to-all-done.x_ref, bf16[256,256]{1,0:T(8,128)(2,1)} %constant.63.clone.sort_ref, bf16[4,512,1024]{2,1,0:T(8,128)(2,1)} %constant.64.clone.w_ref, f32[1024,256]{1,0:T(8,128)} %constant.65.clone.br_ref, ...), custom_call_target="tpu_custom_call" | custom-call | flops 2147483648 | bytes 2097152 | tf_op jit(solution)/shard_map/first_pass/pallas_call | solution.py:98
  76.1 5.4 %all-to-all-done.1.z_ref.refs_1_ = bf16[8,4,64,256]{3,2,1,0:T(8,128)(2,1)S(1)} async-done(((bf16[8,4,64,256]{3,2,1,0:T(8,128)(2,1)}), bf16[8,4,64,256]{3,2,1,0:T(8,128)(2,1)S(1)}, u32[]{:S(2)}, u32[]{:S(2)}) %all-to-all-start.1) | async-done | bytes 1048608 | tf_op jit(solution)/shard_map/all_to_all | solution.py:291
  81.6 3.6 %all-to-all-start.2 = ((bf16[8,4,64,256]{3,2,1,0:T(8,128)(2,1)}), bf16[8,4,64,256]{3,2,1,0:T(8,128)(2,1)S(1)}, u32[]{:S(2)}, u32[]{:S(2)}) async-start(bf16[8,4,64,256]{3,2,1,0:T(8,128)(2,1)} %gate.1), calls=%async_computation.2 | async-start | bytes 2097152 | tf_op jit(solution)/shard_map/all_to_all | solution.py:292
  85.1 0.1 stack.39.place_ref
  85.2 6.0 %fstat_pass.2 = (bf16[64,2048]{1,0:T(8,128)(2,1)S(1)}, bf16[16,1024]{1,0:T(8,128)(2,1)S(1)}, bf16[16,1024]{1,0:T(8,128)(2,1)S(1)}) custom-call(s32[5]{0:T(128)S(1)} %stack.39.place_ref, f32[2,3]{1,0:T(2,128)S(1)} %copy-done.5, bf16[8,4,64,256]{3,2,1,0:T(8,128)(2,1)S(1)} %all-to-all-done.1.z_ref.refs_1_, bf16[4,4,1024,256]{3,2,1,0:T(8,128)(2,1)} %constant.67.clone.w_ref), custom_call_target="tpu_custom_call" | custom-call | flops 2147483648 | bytes 8388608 | tf_op jit(solution)/shard_map/fstat_pass/pallas_call | solution.py:167
  91.3 0.0 copy-start.6
  91.3 2.7 %collective-permute-start = (bf16[64,2048]{1,0:T(8,128)(2,1)S(1)}, bf16[64,2048]{1,0:T(8,128)(2,1)S(1)}, u32[]{:S(2)}, u32[]{:S(2)}) collective-permute-start(bf16[64,2048]{1,0:T(8,128)(2,1)S(1)} %get-tuple-element.11.refs_0_), channel_id=1, source_target_pairs={{0,8},{1,9},{2,10},{3,11},{4,12},{5,13},{6,14},{7,15},{8,0},{9,1},... | collective-permute-start | bytes 786440 | tf_op jit(solution)/shard_map/ppermute | solution.py:287
  94.0 11.2 %all-to-all-done.2.z_ref = bf16[8,4,64,256]{3,2,1,0:T(8,128)(2,1)S(1)} async-done(((bf16[8,4,64,256]{3,2,1,0:T(8,128)(2,1)}), bf16[8,4,64,256]{3,2,1,0:T(8,128)(2,1)S(1)}, u32[]{:S(2)}, u32[]{:S(2)}) %all-to-all-start.2) | async-done | bytes 1048608 | tf_op jit(solution)/shard_map/all_to_all | solution.py:292
  105.1 6.0 %fstat_pass.3 = (f32[64,2048]{1,0:T(8,128)S(1)}, f32[16,1024]{1,0:T(8,128)S(1)}, f32[16,1024]{1,0:T(8,128)S(1)}) custom-call(s32[5]{0:T(128)S(1)} %stack.39.place_ref, f32[2,3]{1,0:T(2,128)S(1)} %copy-done.5, bf16[8,4,64,256]{3,2,1,0:T(8,128)(2,1)S(1)} %all-to-all-done.2.z_ref, bf16[4,4,1024,256]{3,2,1,0:T(8,128)(2,1)} %constant.67.clone.w_ref, ...), custom_call_target="tpu_custom_call" | custom-call | flops 2147483648 | bytes 8388608 | tf_op jit(solution)/shard_map/fstat_pass/pallas_call | solution.py:167
  111.2 0.1 collective-permute-start.3
  111.2 4.4 %collective-permute-start.4 = (f32[16,1024]{1,0:T(8,128)S(1)}, f32[16,1024]{1,0:T(8,128)S(1)}, u32[]{:S(2)}, u32[]{:S(2)}) collective-permute-start(f32[16,1024]{1,0:T(8,128)S(1)} %get-tuple-element.16), channel_id=1, source_target_pairs={{0,15},{1,0},{2,1},{3,2},{4,3},{5,4},{6,5},{7,6},{8,7},{9,8},{10,9... | collective-permute-start | bytes 196616 | tf_op jit(solution)/shard_map/ppermute | solution.py:287
  115.7 0.0 collective-permute-start.1
  115.7 2.6 %collective-permute-start.2 = (bf16[16,1024]{1,0:T(8,128)(2,1)S(1)}, bf16[16,1024]{1,0:T(8,128)(2,1)S(1)}, u32[]{:S(2)}, u32[]{:S(2)}) collective-permute-start(bf16[16,1024]{1,0:T(8,128)(2,1)S(1)} %get-tuple-element.14), channel_id=1, source_target_pairs={{0,7},{1,8},{2,9},{3,10},{4,11},{5,12},{6,13},{7,14},{8,15},{9,0},... | collective-permute-start | bytes 98312 | tf_op jit(solution)/shard_map/ppermute | solution.py:287
  118.3 0.0 copy-done.6
  118.3 0.1 copy.13.offsets_ref
  118.4 1.5 %collective-permute-done.1.refs_0_ = bf16[16,1024]{1,0:T(8,128)(2,1)S(1)} collective-permute-done((bf16[16,1024]{1,0:T(8,128)(2,1)S(1)}, bf16[16,1024]{1,0:T(8,128)(2,1)S(1)}, u32[]{:S(2)}, u32[]{:S(2)}) %collective-permute-start.1) | collective-permute-done | bytes 32800 | tf_op jit(solution)/shard_map/ppermute | solution.py:287
  119.9 0.3 collective-permute-done.2.refs_1_
  120.2 0.0 collective-permute-done.other_ref
  120.2 0.0 collective-permute-done.3.refs_2_
  120.2 0.0 collective-permute-done.4.refs_3_
  120.2 3.4 %detect.1 = f32[8,64,2048]{2,1,0:T(8,128)} custom-call(s32[8,2]{1,0:T(8,128)S(1)} %copy.13.offsets_ref, s32[5]{0:T(128)S(1)} %stack.39.place_ref, bf16[64,2048]{1,0:T(8,128)(2,1)S(1)} %collective-permute-done.other_ref, f32[64,2048]{1,0:T(8,128)S(1)} %get-tuple-element.12.own_ref, bf16[16,1024]{1,0:T(8,128)(2,1)S(1)} %collective-permute-done.1.refs_0_, ...), custom_call_target="tpu_custom_call" | custom-call | flops 3145728 | bytes 4194304 | tf_op jit(solution)/shard_map/detect/pallas_call | solution.py:242
  (10 shorter events, 0.0 us)
Async XLA Ops:
  2.6 48.5 %all-to-all-start = ((bf16[16,4,64,256]{3,2,1,0:T(8,128)(2,1)}), bf16[16,4,64,256]{3,2,1,0:T(8,128)(2,1)S(1)}, u32[]{:S(2)}, u32[]{:S(2)}) async-start(bf16[16,4,64,256]{3,2,1,0:T(8,128)(2,1)} %pack.1), calls=%async_computation | async-start | bytes 4194304 | tf_op jit(solution)/shard_map/all_to_all | solution.py:281
  13.9 42.9 %copy-start.1 = (f32[1024,1]{1,0:T(8,128)}, f32[1024,1]{1,0:T(8,128)S(1)}, u32[]{:S(2)}) copy-start(f32[1024,1]{1,0:T(8,128)S(1)} %get-tuple-element.17.vi_ref) | copy-start | bytes 12292
  13.9 42.9 %copy-start.3 = (f32[1024,1]{1,0:T(8,128)}, f32[1024,1]{1,0:T(8,128)S(1)}, u32[]{:S(2)}) copy-start(f32[1024,1]{1,0:T(8,128)S(1)} %get-tuple-element.18.vr_ref) | copy-start | bytes 12292
  56.8 24.7 %all-to-all-start.1 = ((bf16[8,4,64,256]{3,2,1,0:T(8,128)(2,1)}), bf16[8,4,64,256]{3,2,1,0:T(8,128)(2,1)S(1)}, u32[]{:S(2)}, u32[]{:S(2)}) async-start(bf16[8,4,64,256]{3,2,1,0:T(8,128)(2,1)} %first_pass.2.refs_0_), calls=%async_computation.1 | async-start | bytes 2097152 | tf_op jit(solution)/shard_map/all_to_all | solution.py:291
  67.1 1.3 %copy-start = (bf16[8,4,64,256]{3,2,1,0:T(8,128)(2,1)S(1)}, bf16[8,4,64,256]{3,2,1,0:T(8,128)(2,1)}, u32[]{:S(2)}) copy-start(bf16[8,4,64,256]{3,2,1,0:T(8,128)(2,1)} %first_pass.2.refs_0_) | copy-start | bytes 3145732
  68.4 1.0 copy-start.2
  69.4 1.0 copy-start.4
  76.1 9.1 %copy-start.5 = (f32[2,3]{1,0:T(2,128)S(1)}, f32[2,3]{1,0:T(2,128)}, u32[]{:S(2)}) copy-start(f32[2,3]{1,0:T(2,128)} %coef_ref.3) | copy-start | bytes 76
  81.6 23.6 %all-to-all-start.2 = ((bf16[8,4,64,256]{3,2,1,0:T(8,128)(2,1)}), bf16[8,4,64,256]{3,2,1,0:T(8,128)(2,1)S(1)}, u32[]{:S(2)}, u32[]{:S(2)}) async-start(bf16[8,4,64,256]{3,2,1,0:T(8,128)(2,1)} %gate.1), calls=%async_computation.2 | async-start | bytes 2097152 | tf_op jit(solution)/shard_map/all_to_all | solution.py:292
  91.3 27.0 %copy-start.6 = (s32[8,2]{0,1:T(2,128)S(1)}, s32[8,2]{0,1:T(2,128)}, u32[]{:S(2)}) copy-start(s32[8,2]{0,1:T(2,128)} %param.11) | copy-start | bytes 196
  91.3 28.9 %collective-permute-start = (bf16[64,2048]{1,0:T(8,128)(2,1)S(1)}, bf16[64,2048]{1,0:T(8,128)(2,1)S(1)}, u32[]{:S(2)}, u32[]{:S(2)}) collective-permute-start(bf16[64,2048]{1,0:T(8,128)(2,1)S(1)} %get-tuple-element.11.refs_0_), channel_id=1, source_target_pairs={{0,8},{1,9},{2,10},{3,11},{4,12},{5,13},{6,14},{7,15},{8,0},{9,1},... | collective-permute-start | bytes 786440 | tf_op jit(solution)/shard_map/ppermute | solution.py:287
  111.2 9.0 %collective-permute-start.3 = (f32[16,1024]{1,0:T(8,128)S(1)}, f32[16,1024]{1,0:T(8,128)S(1)}, u32[]{:S(2)}, u32[]{:S(2)}) collective-permute-start(f32[16,1024]{1,0:T(8,128)S(1)} %get-tuple-element.15), channel_id=1, source_target_pairs={{0,1},{1,2},{2,3},{3,4},{4,5},{5,6},{6,7},{7,8},{8,9},{9,10},{10,1... | collective-permute-start | bytes 196616 | tf_op jit(solution)/shard_map/ppermute | solution.py:287
  111.2 8.9 %collective-permute-start.4 = (f32[16,1024]{1,0:T(8,128)S(1)}, f32[16,1024]{1,0:T(8,128)S(1)}, u32[]{:S(2)}, u32[]{:S(2)}) collective-permute-start(f32[16,1024]{1,0:T(8,128)S(1)} %get-tuple-element.16), channel_id=1, source_target_pairs={{0,15},{1,0},{2,1},{3,2},{4,3},{5,4},{6,5},{7,6},{8,7},{9,8},{10,9... | collective-permute-start | bytes 196616 | tf_op jit(solution)/shard_map/ppermute | solution.py:287
  115.7 4.2 %collective-permute-start.1 = (bf16[16,1024]{1,0:T(8,128)(2,1)S(1)}, bf16[16,1024]{1,0:T(8,128)(2,1)S(1)}, u32[]{:S(2)}, u32[]{:S(2)}) collective-permute-start(bf16[16,1024]{1,0:T(8,128)(2,1)S(1)} %get-tuple-element.13), channel_id=1, source_target_pairs={{0,9},{1,10},{2,11},{3,12},{4,13},{5,14},{6,15},{7,0},{8,1},{9,2},... | collective-permute-start | bytes 98312 | tf_op jit(solution)/shard_map/ppermute | solution.py:287
  115.7 4.5 %collective-permute-start.2 = (bf16[16,1024]{1,0:T(8,128)(2,1)S(1)}, bf16[16,1024]{1,0:T(8,128)(2,1)S(1)}, u32[]{:S(2)}, u32[]{:S(2)}) collective-permute-start(bf16[16,1024]{1,0:T(8,128)(2,1)S(1)} %get-tuple-element.14), channel_id=1, source_target_pairs={{0,7},{1,8},{2,9},{3,10},{4,11},{5,12},{6,13},{7,14},{8,15},{9,0},... | collective-permute-start | bytes 98312 | tf_op jit(solution)/shard_map/ppermute | solution.py:287
where the time goes:
time: 124 us
  waiting for transfers between devices  55.6 us (45%)
  starting transfers between devices  31 us (25%)
  Pallas kernels  29.5 us (24%)
  local copies, waits for them, and re-layouts  4.55 us (4%)
  other arithmetic  2.85 us (2%)
    all_to_all x1, waiting for transfers between devices, local(): pieces = trade(pack(series, groups))  37.2 us
    pallas_call x2, Pallas kernels, fstat_pass(): pl.pallas_call(functools.partial(fstat_kernel, length), grid=(table.shape...  12.1 us
    pallas_call x2, Pallas kernels, first_pass(): pl.pallas_call(first_kernel, grid_spec=pltpu.PrefetchScalarGridSpec(num_s...  11.4 us
    all_to_all x1, waiting for transfers between devices, local(): near = trade(gate(near, far), axis_index_groups=halves)  11.2 us
    all_to_all x1, starting transfers between devices, local(): far = trade(far, axis_index_groups=halves)  10.3 us
    ppermute x5, starting transfers between devices, move(): lax.ppermute(x, 'tm', [(i, (i + by) % devices) for i in range(devices)])  9.81 us
    all_to_all x1, starting transfers between devices, local(): pieces = trade(pack(series, groups))  7.39 us
    all_to_all x1, waiting for transfers between devices, local(): far = trade(far, axis_index_groups=halves)  5.43 us
  transfers between devices with their start and end apart: 8, of which 5 were waited for; matrix products, arithmetic and copies ran while one was open for 3% of the time, Pallas kernels for 14%

commit v1 on v0

--- a/solution.py
+++ b/solution.py
@@ -177,17 +177,17 @@
     )(place, antenna, z, in_hbm(table), *after)
 
 
-def gate(x, after):
+def gate(x, *after):
     return pl.pallas_call(
         lambda *refs: None,
-        in_specs=[ANY, ANY],
+        in_specs=[ANY] * (1 + len(after)),
         out_specs=ANY,
         out_shape=pltpu.HBM(x.shape, x.dtype),
         input_output_aliases={0: 0},
         compiler_params=params(2),
         cost_estimate=cost(0, 0),
         name="gate",
-    )(in_hbm(x), after)
+    )(in_hbm(x), *after)
 
 
 def detect_kernel(offsets_ref, place_ref, other_ref, own_ref, *refs):
@@ -291,9 +291,10 @@
     far = trade(far, axis_index_groups=halves)
     near = trade(gate(near, far), axis_index_groups=halves)
     far, far_tail, far_head = fstat_pass(far, place, long, antenna, length, BF16)
+    early = [move(far_tail, groups + 1), move(far_head, groups - 1)]
+    far = gate(far, *early)
     other = move(far, groups)
     own, tail, head = fstat_pass(near, place, long, antenna, length, F32, (far,))
-    early = [move(far_tail, groups + 1), move(far_head, groups - 1)]
     late = [move(tail, 1), move(head, -1)]
     return detect(offsets, place, other, own, early, late)
 

time: 124 us -> 121 us (0.976)
  waiting for transfers between devices: 55.6 us -> 51.5 us
  local copies, waits for them, and re-layouts: 4.55 us -> 6.24 us
    all_to_all x1, waiting for transfers between devices: 11.2 us -> 0.01 us  [local(): near = trade(gate(near, far), axis_index_groups=halves)]
    ppermute x5, waiting for transfers between devices: 1.78 us -> 8.95 us  [move(): lax.ppermute(x, 'tm', [(i, (i + by) % devices) for i in range(devices)])]
    unnamed x15 -> x19, local copies, waits for them, and re-layouts: 3.44 us -> 5.11 us
  transfers between devices with their start and end apart: 8 -> 8, of which waited for: 5 -> 5; matrix products, arithmetic and copies ran while one was open for 3% -> 3% of each run, Pallas kernels for 14% -> 15%
where the time goes in v1:
time: 121 us; the launch traced here: 120 us
  waiting for transfers between devices  51.5 us (43%)
  starting transfers between devices  30 us (25%)
  Pallas kernels  29.5 us (24%)
  local copies, waits for them, and re-layouts  6.24 us (5%)
  other arithmetic  2.85 us (2%)
    all_to_all x1, waiting for transfers between devices, local(): pieces = trade(pack(series, groups))  37.2 us
    pallas_call x2, Pallas kernels, fstat_pass(): pl.pallas_call(functools.partial(fstat_kernel, length), grid=(table.shape...  12.1 us
    pallas_call x2, Pallas kernels, first_pass(): pl.pallas_call(first_kernel, grid_spec=pltpu.PrefetchScalarGridSpec(num_s...  11.4 us
    all_to_all x1, starting transfers between devices, local(): far = trade(far, axis_index_groups=halves)  10.3 us
    ppermute x5, waiting for transfers between devices, move(): lax.ppermute(x, 'tm', [(i, (i + by) % devices) for i in range(devices)])  8.95 us
    ppermute x5, starting transfers between devices, move(): lax.ppermute(x, 'tm', [(i, (i + by) % devices) for i in range(devices)])  8.83 us
    all_to_all x1, starting transfers between devices, local(): pieces = trade(pack(series, groups))  7.39 us
    all_to_all x1, waiting for transfers between devices, local(): far = trade(far, axis_index_groups=halves)  5.43 us
  transfers between devices with their start and end apart: 8, of which 5 were waited for; matrix products, arithmetic and copies ran while one was open for 3% of the time, Pallas kernels for 15%

profile of v1, /device:TPU:0, one launch (start us, length us, event | category | flops | bytes accessed | tf_op | source)
XLA Modules:
  0.0 120.3 jit_solution(18289353375055791122)
XLA Ops:
  0.0 2.6 %pack.1 = bf16[16,4,64,256]{3,2,1,0:T(8,128)(2,1)} custom-call(bf16[2,4,64,2048]{3,2,1,0:T(8,128)(2,1)} %x_ref.1), custom_call_target="tpu_custom_call" | custom-call | bytes 4194304 | tf_op jit(solution)/shard_map/pack/pallas_call | solution.py:53
  2.6 7.4 %all-to-all-start = ((bf16[16,4,64,256]{3,2,1,0:T(8,128)(2,1)}), bf16[16,4,64,256]{3,2,1,0:T(8,128)(2,1)S(1)}, u32[]{:S(2)}, u32[]{:S(2)}) async-start(bf16[16,4,64,256]{3,2,1,0:T(8,128)(2,1)} %pack.1), calls=%async_computation | async-start | bytes 4194304 | tf_op jit(solution)/shard_map/all_to_all | solution.py:281
  10.1 1.0 copy.13
  11.1 2.8 %sine_negate_fusion = (f32[1024,1]{1,0:T(8,128)S(1)}, f32[1024,1]{1,0:T(8,128)S(1)}) fusion(f32[1024,1]{1,0:T(8,128)} %copy.13), kind=kLoop, calls=%fused_computation | loop fusion | flops 2048 | bytes 12288 | tf_op jit(solution)/shard_map/neg | solution.py:277
  14.0 37.2 %all-to-all-done.x_ref = bf16[16,4,64,256]{3,2,1,0:T(8,128)(2,1)S(1)} async-done(((bf16[16,4,64,256]{3,2,1,0:T(8,128)(2,1)}), bf16[16,4,64,256]{3,2,1,0:T(8,128)(2,1)S(1)}, u32[]{:S(2)}, u32[]{:S(2)}) %all-to-all-start) | async-done | bytes 2097184 | tf_op jit(solution)/shard_map/all_to_all | solution.py:281
  51.1 5.7 %first_pass.2.refs_0_ = bf16[8,4,64,256]{3,2,1,0:T(8,128)(2,1)} custom-call(s32[1]{0:T(128)} %bitcast.5.half_ref, bf16[16,4,64,256]{3,2,1,0:T(8,128)(2,1)S(1)} %all-to-all-done.x_ref, bf16[256,256]{1,0:T(8,128)(2,1)} %constant.63.clone.sort_ref, bf16[4,512,1024]{2,1,0:T(8,128)(2,1)} %constant.64.clone.w_ref, f32[1024,256]{1,0:T(8,128)} %constant.65.clone.br_ref, ...), custom_call_target="tpu_custom_call" | custom-call | flops 2147483648 | bytes 2097152 | tf_op jit(solution)/shard_map/first_pass/pallas_call | solution.py:98
  56.8 10.3 %all-to-all-start.1 = ((bf16[8,4,64,256]{3,2,1,0:T(8,128)(2,1)}), bf16[8,4,64,256]{3,2,1,0:T(8,128)(2,1)S(1)}, u32[]{:S(2)}, u32[]{:S(2)}) async-start(bf16[8,4,64,256]{3,2,1,0:T(8,128)(2,1)} %first_pass.2.refs_0_), calls=%async_computation.1 | async-start | bytes 2097152 | tf_op jit(solution)/shard_map/all_to_all | solution.py:291
  67.1 1.3 %copy-done = bf16[8,4,64,256]{3,2,1,0:T(8,128)(2,1)S(1)} copy-done((bf16[8,4,64,256]{3,2,1,0:T(8,128)(2,1)S(1)}, bf16[8,4,64,256]{3,2,1,0:T(8,128)(2,1)}, u32[]{:S(2)}) %copy-start) | copy-done | bytes 1048600
  68.4 1.0 copy-done.2
  69.4 1.0 copy-done.4
  70.4 5.7 %first_pass.3.refs_0_ = bf16[8,4,64,256]{3,2,1,0:T(8,128)(2,1)} custom-call(s32[1]{0:T(128)} %bitcast.half_ref, bf16[16,4,64,256]{3,2,1,0:T(8,128)(2,1)S(1)} %all-to-all-done.x_ref, bf16[256,256]{1,0:T(8,128)(2,1)} %constant.63.clone.sort_ref, bf16[4,512,1024]{2,1,0:T(8,128)(2,1)} %constant.64.clone.w_ref, f32[1024,256]{1,0:T(8,128)} %constant.65.clone.br_ref, ...), custom_call_target="tpu_custom_call" | custom-call | flops 2147483648 | bytes 2097152 | tf_op jit(solution)/shard_map/first_pass/pallas_call | solution.py:98
  76.1 5.4 %all-to-all-done.1.z_ref.refs_1_ = bf16[8,4,64,256]{3,2,1,0:T(8,128)(2,1)S(1)} async-done(((bf16[8,4,64,256]{3,2,1,0:T(8,128)(2,1)}), bf16[8,4,64,256]{3,2,1,0:T(8,128)(2,1)S(1)}, u32[]{:S(2)}, u32[]{:S(2)}) %all-to-all-start.1) | async-done | bytes 1048608 | tf_op jit(solution)/shard_map/all_to_all | solution.py:291
  81.6 3.6 %all-to-all-start.2 = ((bf16[8,4,64,256]{3,2,1,0:T(8,128)(2,1)}), bf16[8,4,64,256]{3,2,1,0:T(8,128)(2,1)S(1)}, u32[]{:S(2)}, u32[]{:S(2)}) async-start(bf16[8,4,64,256]{3,2,1,0:T(8,128)(2,1)} %gate.3), calls=%async_computation.2 | async-start | bytes 2097152 | tf_op jit(solution)/shard_map/all_to_all | solution.py:292
  85.1 0.1 stack.39.place_ref
  85.2 6.0 %fstat_pass.2 = (bf16[64,2048]{1,0:T(8,128)(2,1)S(1)}, bf16[16,1024]{1,0:T(8,128)(2,1)S(1)}, bf16[16,1024]{1,0:T(8,128)(2,1)S(1)}) custom-call(s32[5]{0:T(128)S(1)} %stack.39.place_ref, f32[2,3]{1,0:T(2,128)S(1)} %copy-done.7, bf16[8,4,64,256]{3,2,1,0:T(8,128)(2,1)S(1)} %all-to-all-done.1.z_ref.refs_1_, bf16[4,4,1024,256]{3,2,1,0:T(8,128)(2,1)} %constant.67.clone.w_ref), custom_call_target="tpu_custom_call" | custom-call | flops 2147483648 | bytes 8388608 | tf_op jit(solution)/shard_map/fstat_pass/pallas_call | solution.py:167
  91.3 0.0 copy-start.5
  91.3 0.7 copy-done.5
  92.0 2.6 %collective-permute-start = (bf16[16,1024]{1,0:T(8,128)(2,1)S(1)}, bf16[16,1024]{1,0:T(8,128)(2,1)S(1)}, u32[]{:S(2)}, u32[]{:S(2)}) collective-permute-start(bf16[16,1024]{1,0:T(8,128)(2,1)S(1)} %get-tuple-element.12), channel_id=1, source_target_pairs={{0,9},{1,10},{2,11},{3,12},{4,13},{5,14},{6,15},{7,0},{8,1},{9,2},... | collective-permute-start | bytes 98312 | tf_op jit(solution)/shard_map/ppermute | solution.py:287
  94.5 0.1 collective-permute-start.1
  94.6 7.1 %collective-permute-done.refs_1_.refs_0_ = bf16[16,1024]{1,0:T(8,128)(2,1)S(1)} collective-permute-done((bf16[16,1024]{1,0:T(8,128)(2,1)S(1)}, bf16[16,1024]{1,0:T(8,128)(2,1)S(1)}, u32[]{:S(2)}, u32[]{:S(2)}) %collective-permute-start) | collective-permute-done | bytes 32800 | tf_op jit(solution)/shard_map/ppermute | solution.py:287
  101.7 0.0 collective-permute-done.1.refs_2_.refs_1_
  101.7 1.7 %collective-permute-start.2 = (bf16[64,2048]{1,0:T(8,128)(2,1)}, bf16[64,2048]{1,0:T(8,128)(2,1)S(1)}, u32[]{:S(2)}, u32[]{:S(2)}) collective-permute-start(bf16[64,2048]{1,0:T(8,128)(2,1)} %gate.2.refs_0_), channel_id=1, source_target_pairs={{0,8},{1,9},{2,10},{3,11},{4,12},{5,13},{6,14},{7,15},{8,0},{9,1},... | collective-permute-start | bytes 786440 | tf_op jit(solution)/shard_map/ppermute | solution.py:287
  103.4 0.0 all-to-all-done.2.z_ref
  103.4 1.0 copy-done.6
  104.4 6.0 %fstat_pass.3 = (f32[64,2048]{1,0:T(8,128)S(1)}, f32[16,1024]{1,0:T(8,128)S(1)}, f32[16,1024]{1,0:T(8,128)S(1)}) custom-call(s32[5]{0:T(128)S(1)} %stack.39.place_ref, f32[2,3]{1,0:T(2,128)S(1)} %copy-done.7, bf16[8,4,64,256]{3,2,1,0:T(8,128)(2,1)S(1)} %all-to-all-done.2.z_ref, bf16[4,4,1024,256]{3,2,1,0:T(8,128)(2,1)} %constant.67.clone.w_ref, ...), custom_call_target="tpu_custom_call" | custom-call | flops 2147483648 | bytes 8388608 | tf_op jit(solution)/shard_map/fstat_pass/pallas_call | solution.py:167
  110.4 0.1 collective-permute-start.3
  110.5 4.4 %collective-permute-start.4 = (f32[16,1024]{1,0:T(8,128)S(1)}, f32[16,1024]{1,0:T(8,128)S(1)}, u32[]{:S(2)}, u32[]{:S(2)}) collective-permute-start(f32[16,1024]{1,0:T(8,128)S(1)} %get-tuple-element.16), channel_id=1, source_target_pairs={{0,15},{1,0},{2,1},{3,2},{4,3},{5,4},{6,5},{7,6},{8,7},{9,8},{10,9... | collective-permute-start | bytes 196616 | tf_op jit(solution)/shard_map/ppermute | solution.py:287
  114.9 0.1 copy.14.offsets_ref
  115.0 1.3 %collective-permute-done.2.other_ref = bf16[64,2048]{1,0:T(8,128)(2,1)S(1)} collective-permute-done((bf16[64,2048]{1,0:T(8,128)(2,1)}, bf16[64,2048]{1,0:T(8,128)(2,1)S(1)}, u32[]{:S(2)}, u32[]{:S(2)}) %collective-permute-start.2) | collective-permute-done | bytes 262176 | tf_op jit(solution)/shard_map/ppermute | solution.py:287
  116.3 0.6 collective-permute-done.3.refs_2_
  116.9 0.0 collective-permute-done.4.refs_3_
  116.9 3.4 %detect.1 = f32[8,64,2048]{2,1,0:T(8,128)} custom-call(s32[8,2]{1,0:T(8,128)S(1)} %copy.14.offsets_ref, s32[5]{0:T(128)S(1)} %stack.39.place_ref, bf16[64,2048]{1,0:T(8,128)(2,1)S(1)} %collective-permute-done.2.other_ref, f32[64,2048]{1,0:T(8,128)S(1)} %get-tuple-element.14.own_ref, bf16[16,1024]{1,0:T(8,128)(2,1)S(1)} %collective-permute-done.refs_1_.refs_0_, ...), custom_call_target="tpu_custom_call" | custom-call | flops 3145728 | bytes 4194304 | tf_op jit(solution)/shard_map/detect/pallas_call | solution.py:242
  (15 shorter events, 0.0 us)
Async XLA Ops:
  2.6 48.5 %all-to-all-start = ((bf16[16,4,64,256]{3,2,1,0:T(8,128)(2,1)}), bf16[16,4,64,256]{3,2,1,0:T(8,128)(2,1)S(1)}, u32[]{:S(2)}, u32[]{:S(2)}) async-start(bf16[16,4,64,256]{3,2,1,0:T(8,128)(2,1)} %pack.1), calls=%async_computation | async-start | bytes 4194304 | tf_op jit(solution)/shard_map/all_to_all | solution.py:281
  13.9 42.9 %copy-start.1 = (f32[1024,1]{1,0:T(8,128)}, f32[1024,1]{1,0:T(8,128)S(1)}, u32[]{:S(2)}) copy-start(f32[1024,1]{1,0:T(8,128)S(1)} %get-tuple-element.17.vi_ref) | copy-start | bytes 12292
  13.9 42.9 %copy-start.3 = (f32[1024,1]{1,0:T(8,128)}, f32[1024,1]{1,0:T(8,128)S(1)}, u32[]{:S(2)}) copy-start(f32[1024,1]{1,0:T(8,128)S(1)} %get-tuple-element.18.vr_ref) | copy-start | bytes 12292
  56.8 24.7 %all-to-all-start.1 = ((bf16[8,4,64,256]{3,2,1,0:T(8,128)(2,1)}), bf16[8,4,64,256]{3,2,1,0:T(8,128)(2,1)S(1)}, u32[]{:S(2)}, u32[]{:S(2)}) async-start(bf16[8,4,64,256]{3,2,1,0:T(8,128)(2,1)} %first_pass.2.refs_0_), calls=%async_computation.1 | async-start | bytes 2097152 | tf_op jit(solution)/shard_map/all_to_all | solution.py:291
  67.1 1.3 %copy-start = (bf16[8,4,64,256]{3,2,1,0:T(8,128)(2,1)S(1)}, bf16[8,4,64,256]{3,2,1,0:T(8,128)(2,1)}, u32[]{:S(2)}) copy-start(bf16[8,4,64,256]{3,2,1,0:T(8,128)(2,1)} %first_pass.2.refs_0_) | copy-start | bytes 3145732
  68.4 1.0 copy-start.2
  69.4 1.0 copy-start.4
  76.1 9.1 %copy-start.7 = (f32[2,3]{1,0:T(2,128)S(1)}, f32[2,3]{1,0:T(2,128)}, u32[]{:S(2)}) copy-start(f32[2,3]{1,0:T(2,128)} %coef_ref.3) | copy-start | bytes 76
  81.6 21.8 %all-to-all-start.2 = ((bf16[8,4,64,256]{3,2,1,0:T(8,128)(2,1)}), bf16[8,4,64,256]{3,2,1,0:T(8,128)(2,1)S(1)}, u32[]{:S(2)}, u32[]{:S(2)}) async-start(bf16[8,4,64,256]{3,2,1,0:T(8,128)(2,1)} %gate.3), calls=%async_computation.2 | async-start | bytes 2097152 | tf_op jit(solution)/shard_map/all_to_all | solution.py:292
  91.3 0.7 copy-start.5
  92.0 9.7 %collective-permute-start = (bf16[16,1024]{1,0:T(8,128)(2,1)S(1)}, bf16[16,1024]{1,0:T(8,128)(2,1)S(1)}, u32[]{:S(2)}, u32[]{:S(2)}) collective-permute-start(bf16[16,1024]{1,0:T(8,128)(2,1)S(1)} %get-tuple-element.12), channel_id=1, source_target_pairs={{0,9},{1,10},{2,11},{3,12},{4,13},{5,14},{6,15},{7,0},{8,1},{9,2},... | collective-permute-start | bytes 98312 | tf_op jit(solution)/shard_map/ppermute | solution.py:287
  94.5 7.2 %collective-permute-start.1 = (bf16[16,1024]{1,0:T(8,128)(2,1)S(1)}, bf16[16,1024]{1,0:T(8,128)(2,1)S(1)}, u32[]{:S(2)}, u32[]{:S(2)}) collective-permute-start(bf16[16,1024]{1,0:T(8,128)(2,1)S(1)} %get-tuple-element.13), channel_id=1, source_target_pairs={{0,7},{1,8},{2,9},{3,10},{4,11},{5,12},{6,13},{7,14},{8,15},{9,0},... | collective-permute-start | bytes 98312 | tf_op jit(solution)/shard_map/ppermute | solution.py:287
  101.7 13.2 %copy-start.8 = (s32[8,2]{0,1:T(2,128)S(1)}, s32[8,2]{0,1:T(2,128)}, u32[]{:S(2)}) copy-start(s32[8,2]{0,1:T(2,128)} %param.11) | copy-start | bytes 196
  101.7 14.6 %collective-permute-start.2 = (bf16[64,2048]{1,0:T(8,128)(2,1)}, bf16[64,2048]{1,0:T(8,128)(2,1)S(1)}, u32[]{:S(2)}, u32[]{:S(2)}) collective-permute-start(bf16[64,2048]{1,0:T(8,128)(2,1)} %gate.2.refs_0_), channel_id=1, source_target_pairs={{0,8},{1,9},{2,10},{3,11},{4,12},{5,13},{6,14},{7,15},{8,0},{9,1},... | collective-permute-start | bytes 786440 | tf_op jit(solution)/shard_map/ppermute | solution.py:287
  103.4 1.0 copy-start.6
  110.4 6.4 %collective-permute-start.3 = (f32[16,1024]{1,0:T(8,128)S(1)}, f32[16,1024]{1,0:T(8,128)S(1)}, u32[]{:S(2)}, u32[]{:S(2)}) collective-permute-start(f32[16,1024]{1,0:T(8,128)S(1)} %get-tuple-element.15), channel_id=1, source_target_pairs={{0,1},{1,2},{2,3},{3,4},{4,5},{5,6},{6,7},{7,8},{8,9},{9,10},{10,1... | collective-permute-start | bytes 196616 | tf_op jit(solution)/shard_map/ppermute | solution.py:287
  110.5 6.4 %collective-permute-start.4 = (f32[16,1024]{1,0:T(8,128)S(1)}, f32[16,1024]{1,0:T(8,128)S(1)}, u32[]{:S(2)}, u32[]{:S(2)}) collective-permute-start(f32[16,1024]{1,0:T(8,128)S(1)} %get-tuple-element.16), channel_id=1, source_target_pairs={{0,15},{1,0},{2,1},{3,2},{4,3},{5,4},{6,5},{7,6},{8,7},{9,8},{10,9... | collective-permute-start | bytes 196616 | tf_op jit(solution)/shard_map/ppermute | solution.py:287

commit v2 on v1

--- a/solution.py
+++ b/solution.py
@@ -121,42 +121,44 @@
 
     @pl.when(step == 0)
     def _():
-        groups, cols = z_ref.shape[0], z_ref.shape[-1] // 2
+        groups, cols = z_ref.shape[0], z_ref.shape[-1] // 4
         for source in range(groups):
-            piece = z_ref[source].reshape(lhs_ref.shape[1], 2 * cols)
-            for parity in range(2):
+            piece = z_ref[source].reshape(lhs_ref.shape[1], 4 * cols)
+            for kind in range(4):
                 at = slice(source * cols, (source + 1) * cols)
-                lhs_ref[parity, :, at] = piece[:, parity * cols : (parity + 1) * cols]
+                lhs_ref[kind, :, at] = piece[:, kind * cols : (kind + 1) * cols]
 
     rows, width = fstat_ref.shape
     tile = w_ref.shape[-1]
-    even, odd = lhs_ref[0], lhs_ref[1]
-    even_real, even_imag = dot(even, w_ref[0, 0]), dot(even, w_ref[0, 1])
-    odd_real, odd_imag = dot(odd, w_ref[0, 2]), dot(odd, w_ref[0, 3])
+    sums = []
+    for kind in range(4):
+        by_real, by_imag = dot(lhs_ref[kind], w_ref[0, kind, 0]), dot(lhs_ref[kind], w_ref[0, kind, 1])
+        part = lambda x, comp: x[comp * rows : (comp + 1) * rows]
+        pairs = [(part(by_real, c) - part(by_imag, c + 1), part(by_imag, c) + part(by_real, c + 1)) for c in (0, 2)]
+        sums.append(pairs[0] + pairs[1])
+    plus = [[x + y for x, y in zip(sums[k], sums[k + 2])] for k in range(2)]
+    minus = [[x - y for x, y in zip(sums[k], sums[k + 2])] for k in range(2)]
+    turned = [minus[1][1], -minus[1][0], minus[1][3], -minus[1][2]]
     coef_a, coef_b, coef_c = [jnp.full((1, tile), coef_ref[place_ref[SEG], at], F32) for at in range(3)]
     scale = 1.0 / ((coef_a * coef_b - coef_c * coef_c) * length)
     coef_a, coef_b, coef_c = coef_a * scale, coef_b * scale, 2.0 * coef_c * scale
-    tails, heads = [], []
-    for half in range(2):
-        by_real = even_real - odd_real if half else even_real + odd_real
-        by_imag = even_imag - odd_imag if half else even_imag + odd_imag
-        part = lambda x, comp: x[comp * rows : (comp + 1) * rows]
-        a_real = part(by_real, 0) - part(by_imag, 1)
-        a_imag = part(by_imag, 0) + part(by_real, 1)
-        b_real = part(by_real, 2) - part(by_imag, 3)
-        b_imag = part(by_imag, 2) + part(by_real, 3)
-        fstat = (
-            coef_b * (a_real * a_real + a_imag * a_imag)
-            + coef_a * (b_real * b_real + b_imag * b_imag)
-            - coef_c * (a_real * b_real + a_imag * b_imag)
-        )
-        tails.append(fstat[rows - DMAX :])
-        heads.append(fstat[:DMAX])
-        at = pl.ds(pl.multiple_of(half * (width // 2) + step * tile, tile), tile)
-        fstat_ref[:, at] = fstat.astype(fstat_ref.dtype)
-    at = pl.ds(pl.multiple_of(step * tile, tile), tile)
-    tail_ref[:, at] = jnp.concatenate(tails, axis=0).astype(tail_ref.dtype)
-    head_ref[:, at] = jnp.concatenate(heads, axis=0).astype(head_ref.dtype)
+    quarter = width // 4
+    for odd, (base, swing) in enumerate(((plus[0], plus[1]), (minus[0], turned))):
+        tails, heads = [], []
+        for half in range(2):
+            a_real, a_imag, b_real, b_imag = [x - y if half else x + y for x, y in zip(base, swing)]
+            fstat = (
+                coef_b * (a_real * a_real + a_imag * a_imag)
+                + coef_a * (b_real * b_real + b_imag * b_imag)
+                - coef_c * (a_real * b_real + a_imag * b_imag)
+            )
+            tails.append(fstat[rows - DMAX :])
+            heads.append(fstat[:DMAX])
+            at = pl.ds(pl.multiple_of((2 * half + odd) * quarter + step * tile, tile), tile)
+            fstat_ref[:, at] = fstat.astype(fstat_ref.dtype)
+        at = pl.ds(pl.multiple_of(odd * quarter + step * tile, tile), tile)
+        tail_ref[:, at] = jnp.concatenate(tails, axis=0).astype(tail_ref.dtype)
+        head_ref[:, at] = jnp.concatenate(heads, axis=0).astype(head_ref.dtype)
 
 
 def fstat_pass(z, place, table, antenna, length, kind, after=()):
@@ -167,12 +169,12 @@
     return pl.pallas_call(
         functools.partial(fstat_kernel, length),
         grid=(table.shape[0],),
-        in_specs=[SMEM, SMEM, VMEM, pl.BlockSpec((1,) + table.shape[1:], lambda t: (t, 0, 0, 0))] + [ANY] * len(after),
+        in_specs=[SMEM, SMEM, VMEM, pl.BlockSpec((1,) + table.shape[1:], lambda t: (t, 0, 0, 0, 0))] + [ANY] * len(after),
         out_specs=[still((rows, width)), still(rim), still(rim)],
         out_shape=[jax.ShapeDtypeStruct((rows, width), kind)] + [jax.ShapeDtypeStruct(rim, kind)] * 2,
-        scratch_shapes=[pltpu.VMEM((2, comps * rows, width // 2), BF16)],
+        scratch_shapes=[pltpu.VMEM((4, comps * rows, width // 4), BF16)],
         compiler_params=params(24),
-        cost_estimate=cost(2 * comps * rows * width * width, 2 * width * width),
+        cost_estimate=cost(comps * rows * width * width, width * width),
         name="fstat_pass",
     )(place, antenna, z, in_hbm(table), *after)
 
@@ -182,12 +184,12 @@
         lambda *refs: None,
         in_specs=[ANY] * (1 + len(after)),
         out_specs=ANY,
-        out_shape=pltpu.HBM(x.shape, x.dtype),
+        out_shape=jax.ShapeDtypeStruct(x.shape, x.dtype),
         input_output_aliases={0: 0},
         compiler_params=params(2),
         cost_estimate=cost(0, 0),
         name="gate",
-    )(in_hbm(x), *after)
+    )(x, *after)
 
 
 def detect_kernel(offsets_ref, place_ref, other_ref, own_ref, *refs):
@@ -267,11 +269,11 @@
     tile = min(256, groups * rows)
     short = np.stack(dft_table(bins, bins, slow)).astype(BF16).reshape(2, -1, tile, slow)
     short = short.transpose(1, 0, 2, 3).reshape(-1, 2 * tile, slow)
-    fast = np.arange(width // 2)
-    tile = min(256, width // 2)
-    long = np.stack([x.astype(BF16) for parity in range(2) for x in dft_table(2 * fast + parity, fast, width)])
-    long = long.reshape(4, width // 2, -1, tile).transpose(2, 0, 1, 3)
-    order = np.concatenate([np.arange(0, cols, 2), np.arange(1, cols, 2)])
+    fast = np.arange(width // 4)
+    tile = min(256, width // 4)
+    long = np.stack([np.stack(dft_table(4 * fast + kind, fast, width)) for kind in range(4)]).astype(BF16)
+    long = long.reshape(4, 2, width // 4, -1, tile).transpose(3, 0, 1, 2, 4)
+    order = np.concatenate([np.arange(kind, cols, 4) for kind in range(4)])
     bases = dft_table(bins, order, length)
     angle = (jnp.arange(slow, dtype=jnp.int32) * (member * cols) % length).astype(F32) * (2.0 * math.pi / length)
     turns = (jnp.cos(angle)[:, None], -jnp.sin(angle)[:, None])

time: 121 us -> 121 us (level)
  waiting for transfers between devices: 51.5 us -> 55.6 us
  Pallas kernels: 29.5 us -> 25.5 us
    ppermute x5, waiting for transfers between devices: 8.95 us -> 13 us  [move(): lax.ppermute(x, 'tm', [(i, (i + by) % devices) for i in range(devices)])]
    pallas_call x2, Pallas kernels: 12.1 us -> 8.05 us  [fstat_pass(): pl.pallas_call(functools.partial(fstat_kernel, length), grid=(table.shape...]
  transfers between devices with their start and end apart: 8 -> 8, of which waited for: 5 -> 4; matrix products, arithmetic and copies ran while one was open for 3% -> 3% of each run, Pallas kernels for 15% -> 11%
where the time goes in v2:
time: 121 us
  waiting for transfers between devices  55.6 us (46%)
  starting transfers between devices  30.1 us (25%)
  Pallas kernels  25.5 us (21%)
  local copies, waits for them, and re-layouts  6.76 us (6%)
  other arithmetic  2.85 us (2%)
    all_to_all x1, waiting for transfers between devices, local(): pieces = trade(pack(series, groups))  37.2 us
    ppermute x5, waiting for transfers between devices, move(): lax.ppermute(x, 'tm', [(i, (i + by) % devices) for i in range(devices)])  13 us
    pallas_call x2, Pallas kernels, first_pass(): pl.pallas_call(first_kernel, grid_spec=pltpu.PrefetchScalarGridSpec(num_s...  11.4 us
    all_to_all x1, starting transfers between devices, local(): far = trade(far, axis_index_groups=halves)  10.3 us
    ppermute x5, starting transfers between devices, move(): lax.ppermute(x, 'tm', [(i, (i + by) % devices) for i in range(devices)])  8.89 us
    pallas_call x2, Pallas kernels, fstat_pass(): pl.pallas_call(functools.partial(fstat_kernel, length), grid=(table.shape...  8.05 us
    all_to_all x1, starting transfers between devices, local(): pieces = trade(pack(series, groups))  7.39 us
    unnamed x19, local copies, waits for them, and re-layouts  5.63 us
  transfers between devices with their start and end apart: 8, of which 4 were waited for; matrix products, arithmetic and copies ran while one was open for 3% of the time, Pallas kernels for 11%

profile of v2, /device:TPU:0, one launch (start us, length us, event | category | flops | bytes accessed | tf_op | source)
XLA Modules:
  0.0 121.0 jit_solution(15054684870578625104)
XLA Ops:
  0.0 2.6 %pack.1 = bf16[16,4,64,256]{3,2,1,0:T(8,128)(2,1)} custom-call(bf16[2,4,64,2048]{3,2,1,0:T(8,128)(2,1)} %x_ref.1), custom_call_target="tpu_custom_call" | custom-call | bytes 4194304 | tf_op jit(solution)/shard_map/pack/pallas_call | solution.py:53
  2.6 7.4 %all-to-all-start = ((bf16[16,4,64,256]{3,2,1,0:T(8,128)(2,1)}), bf16[16,4,64,256]{3,2,1,0:T(8,128)(2,1)S(1)}, u32[]{:S(2)}, u32[]{:S(2)}) async-start(bf16[16,4,64,256]{3,2,1,0:T(8,128)(2,1)} %pack.1), calls=%async_computation | async-start | bytes 4194304 | tf_op jit(solution)/shard_map/all_to_all | solution.py:283
  10.1 1.0 copy.13
  11.1 2.8 %sine_negate_fusion = (f32[1024,1]{1,0:T(8,128)S(1)}, f32[1024,1]{1,0:T(8,128)S(1)}) fusion(f32[1024,1]{1,0:T(8,128)} %copy.13), kind=kLoop, calls=%fused_computation | loop fusion | flops 2048 | bytes 12288 | tf_op jit(solution)/shard_map/neg | solution.py:279
  14.0 37.2 %all-to-all-done.x_ref = bf16[16,4,64,256]{3,2,1,0:T(8,128)(2,1)S(1)} async-done(((bf16[16,4,64,256]{3,2,1,0:T(8,128)(2,1)}), bf16[16,4,64,256]{3,2,1,0:T(8,128)(2,1)S(1)}, u32[]{:S(2)}, u32[]{:S(2)}) %all-to-all-start) | async-done | bytes 2097184 | tf_op jit(solution)/shard_map/all_to_all | solution.py:283
  51.1 5.7 %first_pass.2.refs_0_ = bf16[8,4,64,256]{3,2,1,0:T(8,128)(2,1)} custom-call(s32[1]{0:T(128)} %bitcast.5.half_ref, bf16[16,4,64,256]{3,2,1,0:T(8,128)(2,1)S(1)} %all-to-all-done.x_ref, bf16[256,256]{1,0:T(8,128)(2,1)} %constant.63.clone.sort_ref, bf16[4,512,1024]{2,1,0:T(8,128)(2,1)} %constant.64.clone.w_ref, f32[1024,256]{1,0:T(8,128)} %constant.65.clone.br_ref, ...), custom_call_target="tpu_custom_call" | custom-call | flops 2147483648 | bytes 2097152 | tf_op jit(solution)/shard_map/first_pass/pallas_call | solution.py:98
  56.8 10.3 %all-to-all-start.1 = ((bf16[8,4,64,256]{3,2,1,0:T(8,128)(2,1)}), bf16[8,4,64,256]{3,2,1,0:T(8,128)(2,1)S(1)}, u32[]{:S(2)}, u32[]{:S(2)}) async-start(bf16[8,4,64,256]{3,2,1,0:T(8,128)(2,1)} %first_pass.2.refs_0_), calls=%async_computation.1 | async-start | bytes 2097152 | tf_op jit(solution)/shard_map/all_to_all | solution.py:293
  67.1 1.3 %copy-done.2 = bf16[8,4,64,256]{3,2,1,0:T(8,128)(2,1)S(1)} copy-done((bf16[8,4,64,256]{3,2,1,0:T(8,128)(2,1)S(1)}, bf16[8,4,64,256]{3,2,1,0:T(8,128)(2,1)}, u32[]{:S(2)}) %copy-start.2) | copy-done | bytes 1048600
  68.4 1.0 copy-done.4
  69.4 1.0 copy-done.6
  70.4 5.7 %first_pass.3.refs_0_ = bf16[8,4,64,256]{3,2,1,0:T(8,128)(2,1)} custom-call(s32[1]{0:T(128)} %bitcast.half_ref, bf16[16,4,64,256]{3,2,1,0:T(8,128)(2,1)S(1)} %all-to-all-done.x_ref, bf16[256,256]{1,0:T(8,128)(2,1)} %constant.63.clone.sort_ref, bf16[4,512,1024]{2,1,0:T(8,128)(2,1)} %constant.64.clone.w_ref, f32[1024,256]{1,0:T(8,128)} %constant.65.clone.br_ref, ...), custom_call_target="tpu_custom_call" | custom-call | flops 2147483648 | bytes 2097152 | tf_op jit(solution)/shard_map/first_pass/pallas_call | solution.py:98
  76.1 5.4 %all-to-all-done.1.z_ref.refs_1_ = bf16[8,4,64,256]{3,2,1,0:T(8,128)(2,1)S(1)} async-done(((bf16[8,4,64,256]{3,2,1,0:T(8,128)(2,1)}), bf16[8,4,64,256]{3,2,1,0:T(8,128)(2,1)S(1)}, u32[]{:S(2)}, u32[]{:S(2)}) %all-to-all-start.1) | async-done | bytes 1048608 | tf_op jit(solution)/shard_map/all_to_all | solution.py:293
  81.6 1.2 %copy-done = bf16[8,4,64,256]{3,2,1,0:T(8,128)(2,1)S(1)} copy-done((bf16[8,4,64,256]{3,2,1,0:T(8,128)(2,1)S(1)}, bf16[8,4,64,256]{3,2,1,0:T(8,128)(2,1)}, u32[]{:S(2)}) %copy-start) | copy-done | bytes 1048600
  82.8 1.0 copy-done.1
  83.8 3.6 %all-to-all-start.2 = ((bf16[8,4,64,256]{3,2,1,0:T(8,128)(2,1)}), bf16[8,4,64,256]{3,2,1,0:T(8,128)(2,1)S(1)}, u32[]{:S(2)}, u32[]{:S(2)}) async-start(bf16[8,4,64,256]{3,2,1,0:T(8,128)(2,1)} %copy-done.1), calls=%async_computation.2 | async-start | bytes 2097152 | tf_op jit(solution)/shard_map/all_to_all | solution.py:294
  87.3 0.1 stack.39.place_ref
  87.4 4.0 %fstat_pass.2 = (bf16[64,2048]{1,0:T(8,128)(2,1)S(1)}, bf16[16,1024]{1,0:T(8,128)(2,1)S(1)}, bf16[16,1024]{1,0:T(8,128)(2,1)S(1)}) custom-call(s32[5]{0:T(128)S(1)} %stack.39.place_ref, f32[2,3]{1,0:T(2,128)S(1)} %copy-done.7, bf16[8,4,64,256]{3,2,1,0:T(8,128)(2,1)S(1)} %all-to-all-done.1.z_ref.refs_1_, bf16[2,4,2,512,256]{4,3,2,1,0:T(8,128)(2,1)} %constant.67.clone.w_ref), custom_call_target="tpu_custom_call" | custom-call | flops 1073741824 | bytes 4194304 | tf_op jit(solution)/shard_map/fstat_pass/pallas_call | solution.py:169
  91.5 0.0 copy-start.8
  91.5 2.6 %collective-permute-start = (bf16[16,1024]{1,0:T(8,128)(2,1)S(1)}, bf16[16,1024]{1,0:T(8,128)(2,1)S(1)}, u32[]{:S(2)}, u32[]{:S(2)}) collective-permute-start(bf16[16,1024]{1,0:T(8,128)(2,1)S(1)} %get-tuple-element.12), channel_id=1, source_target_pairs={{0,9},{1,10},{2,11},{3,12},{4,13},{5,14},{6,15},{7,0},{8,1},{9,2},... | collective-permute-start | bytes 98312 | tf_op jit(solution)/shard_map/ppermute | solution.py:289
  94.1 0.1 collective-permute-start.1
  94.2 9.7 %collective-permute-done.refs_1_.refs_0_ = bf16[16,1024]{1,0:T(8,128)(2,1)S(1)} collective-permute-done((bf16[16,1024]{1,0:T(8,128)(2,1)S(1)}, bf16[16,1024]{1,0:T(8,128)(2,1)S(1)}, u32[]{:S(2)}, u32[]{:S(2)}) %collective-permute-start) | collective-permute-done | bytes 32800 | tf_op jit(solution)/shard_map/ppermute | solution.py:289
  103.9 0.0 collective-permute-done.1.refs_2_.refs_1_
  103.9 1.7 %collective-permute-start.2 = (bf16[64,2048]{1,0:T(8,128)(2,1)S(1)}, bf16[64,2048]{1,0:T(8,128)(2,1)S(1)}, u32[]{:S(2)}, u32[]{:S(2)}) collective-permute-start(bf16[64,2048]{1,0:T(8,128)(2,1)S(1)} %gate.2.refs_0_), channel_id=1, source_target_pairs={{0,8},{1,9},{2,10},{3,11},{4,12},{5,13},{6,14},{7,15},{8,0},{9,1},... | collective-permute-start | bytes 786440 | tf_op jit(solution)/shard_map/ppermute | solution.py:289
  105.6 0.0 all-to-all-done.2.z_ref
  105.6 4.0 %fstat_pass.3 = (f32[64,2048]{1,0:T(8,128)S(1)}, f32[16,1024]{1,0:T(8,128)S(1)}, f32[16,1024]{1,0:T(8,128)S(1)}) custom-call(s32[5]{0:T(128)S(1)} %stack.39.place_ref, f32[2,3]{1,0:T(2,128)S(1)} %copy-done.7, bf16[8,4,64,256]{3,2,1,0:T(8,128)(2,1)S(1)} %all-to-all-done.2.z_ref, bf16[2,4,2,512,256]{4,3,2,1,0:T(8,128)(2,1)} %constant.67.clone.w_ref, ...), custom_call_target="tpu_custom_call" | custom-call | flops 1073741824 | bytes 4194304 | tf_op jit(solution)/shard_map/fstat_pass/pallas_call | solution.py:169
  109.6 0.1 collective-permute-start.3
  109.7 4.4 %collective-permute-start.4 = (f32[16,1024]{1,0:T(8,128)S(1)}, f32[16,1024]{1,0:T(8,128)S(1)}, u32[]{:S(2)}, u32[]{:S(2)}) collective-permute-start(f32[16,1024]{1,0:T(8,128)S(1)} %get-tuple-element.16), channel_id=1, source_target_pairs={{0,15},{1,0},{2,1},{3,2},{4,3},{5,4},{6,5},{7,6},{8,7},{9,8},{10,9... | collective-permute-start | bytes 196616 | tf_op jit(solution)/shard_map/ppermute | solution.py:289
  114.1 0.1 copy.14.offsets_ref
  114.2 3.3 %collective-permute-done.2.other_ref = bf16[64,2048]{1,0:T(8,128)(2,1)S(1)} collective-permute-done((bf16[64,2048]{1,0:T(8,128)(2,1)S(1)}, bf16[64,2048]{1,0:T(8,128)(2,1)S(1)}, u32[]{:S(2)}, u32[]{:S(2)}) %collective-permute-start.2) | collective-permute-done | bytes 262176 | tf_op jit(solution)/shard_map/ppermute | solution.py:289
  117.5 0.0 collective-permute-done.3.refs_2_
  117.5 0.0 collective-permute-done.4.refs_3_
  117.5 3.4 %detect.1 = f32[8,64,2048]{2,1,0:T(8,128)} custom-call(s32[8,2]{1,0:T(8,128)S(1)} %copy.14.offsets_ref, s32[5]{0:T(128)S(1)} %stack.39.place_ref, bf16[64,2048]{1,0:T(8,128)(2,1)S(1)} %collective-permute-done.2.other_ref, f32[64,2048]{1,0:T(8,128)S(1)} %get-tuple-element.14.own_ref, bf16[16,1024]{1,0:T(8,128)(2,1)S(1)} %collective-permute-done.refs_1_.refs_0_, ...), custom_call_target="tpu_custom_call" | custom-call | flops 3145728 | bytes 4194304 | tf_op jit(solution)/shard_map/detect/pallas_call | solution.py:244
  (15 shorter events, 0.0 us)
Async XLA Ops:
  2.6 48.5 %all-to-all-start = ((bf16[16,4,64,256]{3,2,1,0:T(8,128)(2,1)}), bf16[16,4,64,256]{3,2,1,0:T(8,128)(2,1)S(1)}, u32[]{:S(2)}, u32[]{:S(2)}) async-start(bf16[16,4,64,256]{3,2,1,0:T(8,128)(2,1)} %pack.1), calls=%async_computation | async-start | bytes 4194304 | tf_op jit(solution)/shard_map/all_to_all | solution.py:283
  13.9 42.9 %copy-start.3 = (f32[1024,1]{1,0:T(8,128)}, f32[1024,1]{1,0:T(8,128)S(1)}, u32[]{:S(2)}) copy-start(f32[1024,1]{1,0:T(8,128)S(1)} %get-tuple-element.17.vi_ref) | copy-start | bytes 12292
  13.9 42.9 %copy-start.5 = (f32[1024,1]{1,0:T(8,128)}, f32[1024,1]{1,0:T(8,128)S(1)}, u32[]{:S(2)}) copy-start(f32[1024,1]{1,0:T(8,128)S(1)} %get-tuple-element.18.vr_ref) | copy-start | bytes 12292
  56.8 24.7 %all-to-all-start.1 = ((bf16[8,4,64,256]{3,2,1,0:T(8,128)(2,1)}), bf16[8,4,64,256]{3,2,1,0:T(8,128)(2,1)S(1)}, u32[]{:S(2)}, u32[]{:S(2)}) async-start(bf16[8,4,64,256]{3,2,1,0:T(8,128)(2,1)} %first_pass.2.refs_0_), calls=%async_computation.1 | async-start | bytes 2097152 | tf_op jit(solution)/shard_map/all_to_all | solution.py:293
  67.1 1.3 %copy-start.2 = (bf16[8,4,64,256]{3,2,1,0:T(8,128)(2,1)S(1)}, bf16[8,4,64,256]{3,2,1,0:T(8,128)(2,1)}, u32[]{:S(2)}) copy-start(bf16[8,4,64,256]{3,2,1,0:T(8,128)(2,1)} %first_pass.2.refs_0_) | copy-start | bytes 3145732
  68.4 1.0 copy-start.4
  69.4 1.0 copy-start.6
  81.6 1.2 %copy-start = (bf16[8,4,64,256]{3,2,1,0:T(8,128)(2,1)S(1)}, bf16[8,4,64,256]{3,2,1,0:T(8,128)(2,1)}, u32[]{:S(2)}) copy-start(bf16[8,4,64,256]{3,2,1,0:T(8,128)(2,1)} %first_pass.3.refs_0_) | copy-start | bytes 3145732
  82.8 4.6 %copy-start.7 = (f32[2,3]{1,0:T(2,128)S(1)}, f32[2,3]{1,0:T(2,128)}, u32[]{:S(2)}) copy-start(f32[2,3]{1,0:T(2,128)} %coef_ref.3) | copy-start | bytes 76
  82.8 1.0 copy-start.1
  83.8 21.8 %all-to-all-start.2 = ((bf16[8,4,64,256]{3,2,1,0:T(8,128)(2,1)}), bf16[8,4,64,256]{3,2,1,0:T(8,128)(2,1)S(1)}, u32[]{:S(2)}, u32[]{:S(2)}) async-start(bf16[8,4,64,256]{3,2,1,0:T(8,128)(2,1)} %copy-done.1), calls=%async_computation.2 | async-start | bytes 2097152 | tf_op jit(solution)/shard_map/all_to_all | solution.py:294
  91.5 22.7 %copy-start.8 = (s32[8,2]{0,1:T(2,128)S(1)}, s32[8,2]{0,1:T(2,128)}, u32[]{:S(2)}) copy-start(s32[8,2]{0,1:T(2,128)} %param.11) | copy-start | bytes 196
  91.5 12.4 %collective-permute-start = (bf16[16,1024]{1,0:T(8,128)(2,1)S(1)}, bf16[16,1024]{1,0:T(8,128)(2,1)S(1)}, u32[]{:S(2)}, u32[]{:S(2)}) collective-permute-start(bf16[16,1024]{1,0:T(8,128)(2,1)S(1)} %get-tuple-element.12), channel_id=1, source_target_pairs={{0,9},{1,10},{2,11},{3,12},{4,13},{5,14},{6,15},{7,0},{8,1},{9,2},... | collective-permute-start | bytes 98312 | tf_op jit(solution)/shard_map/ppermute | solution.py:289
  94.1 9.8 %collective-permute-start.1 = (bf16[16,1024]{1,0:T(8,128)(2,1)S(1)}, bf16[16,1024]{1,0:T(8,128)(2,1)S(1)}, u32[]{:S(2)}, u32[]{:S(2)}) collective-permute-start(bf16[16,1024]{1,0:T(8,128)(2,1)S(1)} %get-tuple-element.13), channel_id=1, source_target_pairs={{0,7},{1,8},{2,9},{3,10},{4,11},{5,12},{6,13},{7,14},{8,15},{9,0},... | collective-permute-start | bytes 98312 | tf_op jit(solution)/shard_map/ppermute | solution.py:289
  103.9 13.6 %collective-permute-start.2 = (bf16[64,2048]{1,0:T(8,128)(2,1)S(1)}, bf16[64,2048]{1,0:T(8,128)(2,1)S(1)}, u32[]{:S(2)}, u32[]{:S(2)}) collective-permute-start(bf16[64,2048]{1,0:T(8,128)(2,1)S(1)} %gate.2.refs_0_), channel_id=1, source_target_pairs={{0,8},{1,9},{2,10},{3,11},{4,12},{5,13},{6,14},{7,15},{8,0},{9,1},... | collective-permute-start | bytes 786440 | tf_op jit(solution)/shard_map/ppermute | solution.py:289
  109.6 7.9 %collective-permute-start.3 = (f32[16,1024]{1,0:T(8,128)S(1)}, f32[16,1024]{1,0:T(8,128)S(1)}, u32[]{:S(2)}, u32[]{:S(2)}) collective-permute-start(f32[16,1024]{1,0:T(8,128)S(1)} %get-tuple-element.15), channel_id=1, source_target_pairs={{0,1},{1,2},{2,3},{3,4},{4,5},{5,6},{6,7},{7,8},{8,9},{9,10},{10,1... | collective-permute-start | bytes 196616 | tf_op jit(solution)/shard_map/ppermute | solution.py:289
  109.7 7.8 %collective-permute-start.4 = (f32[16,1024]{1,0:T(8,128)S(1)}, f32[16,1024]{1,0:T(8,128)S(1)}, u32[]{:S(2)}, u32[]{:S(2)}) collective-permute-start(f32[16,1024]{1,0:T(8,128)S(1)} %get-tuple-element.16), channel_id=1, source_target_pairs={{0,15},{1,0},{2,1},{3,2},{4,3},{5,4},{6,5},{7,6},{8,7},{9,8},{10,9... | collective-permute-start | bytes 196616 | tf_op jit(solution)/shard_map/ppermute | solution.py:289

commit v3 on v2

--- a/solution.py
+++ b/solution.py
@@ -179,12 +179,12 @@
     )(place, antenna, z, in_hbm(table), *after)
 
 
-def gate(x, *after):
+def gate(x, *after, make=jax.ShapeDtypeStruct):
     return pl.pallas_call(
         lambda *refs: None,
         in_specs=[ANY] * (1 + len(after)),
         out_specs=ANY,
-        out_shape=jax.ShapeDtypeStruct(x.shape, x.dtype),
+        out_shape=make(x.shape, x.dtype),
         input_output_aliases={0: 0},
         compiler_params=params(2),
         cost_estimate=cost(0, 0),
@@ -291,7 +291,7 @@
     far = turn(1 - seg)
     near = turn(seg, far)
     far = trade(far, axis_index_groups=halves)
-    near = trade(gate(near, far), axis_index_groups=halves)
+    near = trade(gate(in_hbm(near), far, make=pltpu.HBM), axis_index_groups=halves)
     far, far_tail, far_head = fstat_pass(far, place, long, antenna, length, BF16)
     early = [move(far_tail, groups + 1), move(far_head, groups - 1)]
     far = gate(far, *early)

time: 121 us -> 119 us (0.983)
  local copies, waits for them, and re-layouts: 6.76 us -> 4.55 us
    unnamed x19 -> x15, local copies, waits for them, and re-layouts: 5.63 us -> 3.44 us
  transfers between devices with their start and end apart: 8 -> 8, of which waited for: 4 -> 4; matrix products, arithmetic and copies ran while one was open for 3% -> 3% of each run, Pallas kernels for 11% -> 12%
where the time goes in v3:
time: 119 us
  waiting for transfers between devices  55.7 us (47%)
  starting transfers between devices  30.1 us (25%)
  Pallas kernels  25.5 us (21%)
  local copies, waits for them, and re-layouts  4.55 us (4%)
  other arithmetic  2.85 us (2%)
    all_to_all x1, waiting for transfers between devices, local(): pieces = trade(pack(series, groups))  37.2 us
    ppermute x5, waiting for transfers between devices, move(): lax.ppermute(x, 'tm', [(i, (i + by) % devices) for i in range(devices)])  13 us
    pallas_call x2, Pallas kernels, first_pass(): pl.pallas_call(first_kernel, grid_spec=pltpu.PrefetchScalarGridSpec(num_s...  11.4 us
    all_to_all x1, starting transfers between devices, local(): far = trade(far, axis_index_groups=halves)  10.3 us
    ppermute x5, starting transfers between devices, move(): lax.ppermute(x, 'tm', [(i, (i + by) % devices) for i in range(devices)])  8.89 us
    pallas_call x2, Pallas kernels, fstat_pass(): pl.pallas_call(functools.partial(fstat_kernel, length), grid=(table.shape...  8.05 us
    all_to_all x1, starting transfers between devices, local(): pieces = trade(pack(series, groups))  7.39 us
    all_to_all x1, waiting for transfers between devices, local(): far = trade(far, axis_index_groups=halves)  5.43 us
  transfers between devices with their start and end apart: 8, of which 4 were waited for; matrix products, arithmetic and copies ran while one was open for 3% of the time, Pallas kernels for 12%

profile of v3, /device:TPU:0, one launch (start us, length us, event | category | flops | bytes accessed | tf_op | source)
XLA Modules:
  0.0 118.8 jit_solution(4774730886464885339)
XLA Ops:
  0.0 2.6 %pack.1 = bf16[16,4,64,256]{3,2,1,0:T(8,128)(2,1)} custom-call(bf16[2,4,64,2048]{3,2,1,0:T(8,128)(2,1)} %x_ref.1), custom_call_target="tpu_custom_call" | custom-call | bytes 4194304 | tf_op jit(solution)/shard_map/pack/pallas_call | solution.py:53
  2.6 7.4 %all-to-all-start = ((bf16[16,4,64,256]{3,2,1,0:T(8,128)(2,1)}), bf16[16,4,64,256]{3,2,1,0:T(8,128)(2,1)S(1)}, u32[]{:S(2)}, u32[]{:S(2)}) async-start(bf16[16,4,64,256]{3,2,1,0:T(8,128)(2,1)} %pack.1), calls=%async_computation | async-start | bytes 4194304 | tf_op jit(solution)/shard_map/all_to_all | solution.py:283
  10.1 1.0 copy.13
  11.1 2.8 %sine_negate_fusion = (f32[1024,1]{1,0:T(8,128)S(1)}, f32[1024,1]{1,0:T(8,128)S(1)}) fusion(f32[1024,1]{1,0:T(8,128)} %copy.13), kind=kLoop, calls=%fused_computation | loop fusion | flops 2048 | bytes 12288 | tf_op jit(solution)/shard_map/neg | solution.py:279
  13.9 0.0 copy-start.1
  13.9 37.2 %all-to-all-done.x_ref = bf16[16,4,64,256]{3,2,1,0:T(8,128)(2,1)S(1)} async-done(((bf16[16,4,64,256]{3,2,1,0:T(8,128)(2,1)}), bf16[16,4,64,256]{3,2,1,0:T(8,128)(2,1)S(1)}, u32[]{:S(2)}, u32[]{:S(2)}) %all-to-all-start) | async-done | bytes 2097184 | tf_op jit(solution)/shard_map/all_to_all | solution.py:283
  51.1 5.7 %first_pass.2.refs_0_ = bf16[8,4,64,256]{3,2,1,0:T(8,128)(2,1)} custom-call(s32[1]{0:T(128)} %bitcast.5.half_ref, bf16[16,4,64,256]{3,2,1,0:T(8,128)(2,1)S(1)} %all-to-all-done.x_ref, bf16[256,256]{1,0:T(8,128)(2,1)} %constant.63.clone.sort_ref, bf16[4,512,1024]{2,1,0:T(8,128)(2,1)} %constant.64.clone.w_ref, f32[1024,256]{1,0:T(8,128)} %constant.65.clone.br_ref, ...), custom_call_target="tpu_custom_call" | custom-call | flops 2147483648 | bytes 2097152 | tf_op jit(solution)/shard_map/first_pass/pallas_call | solution.py:98
  56.8 0.0 copy-done.3
  56.8 10.3 %all-to-all-start.1 = ((bf16[8,4,64,256]{3,2,1,0:T(8,128)(2,1)}), bf16[8,4,64,256]{3,2,1,0:T(8,128)(2,1)S(1)}, u32[]{:S(2)}, u32[]{:S(2)}) async-start(bf16[8,4,64,256]{3,2,1,0:T(8,128)(2,1)} %first_pass.2.refs_0_), calls=%async_computation.1 | async-start | bytes 2097152 | tf_op jit(solution)/shard_map/all_to_all | solution.py:293
  67.1 1.3 %copy-done = bf16[8,4,64,256]{3,2,1,0:T(8,128)(2,1)S(1)} copy-done((bf16[8,4,64,256]{3,2,1,0:T(8,128)(2,1)S(1)}, bf16[8,4,64,256]{3,2,1,0:T(8,128)(2,1)}, u32[]{:S(2)}) %copy-start) | copy-done | bytes 1048600
  68.4 1.0 copy-done.2
  69.4 1.0 copy-done.4
  70.4 5.7 %first_pass.3.refs_0_ = bf16[8,4,64,256]{3,2,1,0:T(8,128)(2,1)} custom-call(s32[1]{0:T(128)} %bitcast.half_ref, bf16[16,4,64,256]{3,2,1,0:T(8,128)(2,1)S(1)} %all-to-all-done.x_ref, bf16[256,256]{1,0:T(8,128)(2,1)} %constant.63.clone.sort_ref, bf16[4,512,1024]{2,1,0:T(8,128)(2,1)} %constant.64.clone.w_ref, f32[1024,256]{1,0:T(8,128)} %constant.65.clone.br_ref, ...), custom_call_target="tpu_custom_call" | custom-call | flops 2147483648 | bytes 2097152 | tf_op jit(solution)/shard_map/first_pass/pallas_call | solution.py:98
  76.1 5.4 %all-to-all-done.1.z_ref.refs_1_ = bf16[8,4,64,256]{3,2,1,0:T(8,128)(2,1)S(1)} async-done(((bf16[8,4,64,256]{3,2,1,0:T(8,128)(2,1)}), bf16[8,4,64,256]{3,2,1,0:T(8,128)(2,1)S(1)}, u32[]{:S(2)}, u32[]{:S(2)}) %all-to-all-start.1) | async-done | bytes 1048608 | tf_op jit(solution)/shard_map/all_to_all | solution.py:293
  81.6 3.6 %all-to-all-start.2 = ((bf16[8,4,64,256]{3,2,1,0:T(8,128)(2,1)}), bf16[8,4,64,256]{3,2,1,0:T(8,128)(2,1)S(1)}, u32[]{:S(2)}, u32[]{:S(2)}) async-start(bf16[8,4,64,256]{3,2,1,0:T(8,128)(2,1)} %gate.3), calls=%async_computation.2 | async-start | bytes 2097152 | tf_op jit(solution)/shard_map/all_to_all | solution.py:294
  85.1 0.1 stack.39.place_ref
  85.2 4.0 %fstat_pass.2 = (bf16[64,2048]{1,0:T(8,128)(2,1)S(1)}, bf16[16,1024]{1,0:T(8,128)(2,1)S(1)}, bf16[16,1024]{1,0:T(8,128)(2,1)S(1)}) custom-call(s32[5]{0:T(128)S(1)} %stack.39.place_ref, f32[2,3]{1,0:T(2,128)S(1)} %copy-done.5, bf16[8,4,64,256]{3,2,1,0:T(8,128)(2,1)S(1)} %all-to-all-done.1.z_ref.refs_1_, bf16[2,4,2,512,256]{4,3,2,1,0:T(8,128)(2,1)} %constant.67.clone.w_ref), custom_call_target="tpu_custom_call" | custom-call | flops 1073741824 | bytes 4194304 | tf_op jit(solution)/shard_map/fstat_pass/pallas_call | solution.py:169
  89.3 0.0 copy-start.6
  89.3 2.6 %collective-permute-start = (bf16[16,1024]{1,0:T(8,128)(2,1)S(1)}, bf16[16,1024]{1,0:T(8,128)(2,1)S(1)}, u32[]{:S(2)}, u32[]{:S(2)}) collective-permute-start(bf16[16,1024]{1,0:T(8,128)(2,1)S(1)} %get-tuple-element.12), channel_id=1, source_target_pairs={{0,9},{1,10},{2,11},{3,12},{4,13},{5,14},{6,15},{7,0},{8,1},{9,2},... | collective-permute-start | bytes 98312 | tf_op jit(solution)/shard_map/ppermute | solution.py:289
  91.9 0.1 collective-permute-start.1
  92.0 9.7 %collective-permute-done.refs_1_.refs_0_ = bf16[16,1024]{1,0:T(8,128)(2,1)S(1)} collective-permute-done((bf16[16,1024]{1,0:T(8,128)(2,1)S(1)}, bf16[16,1024]{1,0:T(8,128)(2,1)S(1)}, u32[]{:S(2)}, u32[]{:S(2)}) %collective-permute-start) | collective-permute-done | bytes 32800 | tf_op jit(solution)/shard_map/ppermute | solution.py:289
  101.7 0.0 collective-permute-done.1.refs_2_.refs_1_
  101.7 1.7 %collective-permute-start.2 = (bf16[64,2048]{1,0:T(8,128)(2,1)S(1)}, bf16[64,2048]{1,0:T(8,128)(2,1)S(1)}, u32[]{:S(2)}, u32[]{:S(2)}) collective-permute-start(bf16[64,2048]{1,0:T(8,128)(2,1)S(1)} %gate.2.refs_0_), channel_id=1, source_target_pairs={{0,8},{1,9},{2,10},{3,11},{4,12},{5,13},{6,14},{7,15},{8,0},{9,1},... | collective-permute-start | bytes 786440 | tf_op jit(solution)/shard_map/ppermute | solution.py:289
  103.4 0.0 all-to-all-done.2.z_ref
  103.4 4.0 %fstat_pass.3 = (f32[64,2048]{1,0:T(8,128)S(1)}, f32[16,1024]{1,0:T(8,128)S(1)}, f32[16,1024]{1,0:T(8,128)S(1)}) custom-call(s32[5]{0:T(128)S(1)} %stack.39.place_ref, f32[2,3]{1,0:T(2,128)S(1)} %copy-done.5, bf16[8,4,64,256]{3,2,1,0:T(8,128)(2,1)S(1)} %all-to-all-done.2.z_ref, bf16[2,4,2,512,256]{4,3,2,1,0:T(8,128)(2,1)} %constant.67.clone.w_ref, ...), custom_call_target="tpu_custom_call" | custom-call | flops 1073741824 | bytes 4194304 | tf_op jit(solution)/shard_map/fstat_pass/pallas_call | solution.py:169
  107.4 0.1 collective-permute-start.3
  107.5 4.4 %collective-permute-start.4 = (f32[16,1024]{1,0:T(8,128)S(1)}, f32[16,1024]{1,0:T(8,128)S(1)}, u32[]{:S(2)}, u32[]{:S(2)}) collective-permute-start(f32[16,1024]{1,0:T(8,128)S(1)} %get-tuple-element.16), channel_id=1, source_target_pairs={{0,15},{1,0},{2,1},{3,2},{4,3},{5,4},{6,5},{7,6},{8,7},{9,8},{10,9... | collective-permute-start | bytes 196616 | tf_op jit(solution)/shard_map/ppermute | solution.py:289
  111.9 0.1 copy.14.offsets_ref
  112.0 3.3 %collective-permute-done.2.other_ref = bf16[64,2048]{1,0:T(8,128)(2,1)S(1)} collective-permute-done((bf16[64,2048]{1,0:T(8,128)(2,1)S(1)}, bf16[64,2048]{1,0:T(8,128)(2,1)S(1)}, u32[]{:S(2)}, u32[]{:S(2)}) %collective-permute-start.2) | collective-permute-done | bytes 262176 | tf_op jit(solution)/shard_map/ppermute | solution.py:289
  115.3 0.0 collective-permute-done.3.refs_2_
  115.3 0.0 collective-permute-done.4.refs_3_
  115.3 3.4 %detect.1 = f32[8,64,2048]{2,1,0:T(8,128)} custom-call(s32[8,2]{1,0:T(8,128)S(1)} %copy.14.offsets_ref, s32[5]{0:T(128)S(1)} %stack.39.place_ref, bf16[64,2048]{1,0:T(8,128)(2,1)S(1)} %collective-permute-done.2.other_ref, f32[64,2048]{1,0:T(8,128)S(1)} %get-tuple-element.14.own_ref, bf16[16,1024]{1,0:T(8,128)(2,1)S(1)} %collective-permute-done.refs_1_.refs_0_, ...), custom_call_target="tpu_custom_call" | custom-call | flops 3145728 | bytes 4194304 | tf_op jit(solution)/shard_map/detect/pallas_call | solution.py:244
  (11 shorter events, 0.0 us)
Async XLA Ops:
  2.6 48.5 %all-to-all-start = ((bf16[16,4,64,256]{3,2,1,0:T(8,128)(2,1)}), bf16[16,4,64,256]{3,2,1,0:T(8,128)(2,1)S(1)}, u32[]{:S(2)}, u32[]{:S(2)}) async-start(bf16[16,4,64,256]{3,2,1,0:T(8,128)(2,1)} %pack.1), calls=%async_computation | async-start | bytes 4194304 | tf_op jit(solution)/shard_map/all_to_all | solution.py:283
  13.9 42.9 %copy-start.1 = (f32[1024,1]{1,0:T(8,128)}, f32[1024,1]{1,0:T(8,128)S(1)}, u32[]{:S(2)}) copy-start(f32[1024,1]{1,0:T(8,128)S(1)} %get-tuple-element.17.vi_ref) | copy-start | bytes 12292
  13.9 42.9 %copy-start.3 = (f32[1024,1]{1,0:T(8,128)}, f32[1024,1]{1,0:T(8,128)S(1)}, u32[]{:S(2)}) copy-start(f32[1024,1]{1,0:T(8,128)S(1)} %get-tuple-element.18.vr_ref) | copy-start | bytes 12292
  56.8 24.7 %all-to-all-start.1 = ((bf16[8,4,64,256]{3,2,1,0:T(8,128)(2,1)}), bf16[8,4,64,256]{3,2,1,0:T(8,128)(2,1)S(1)}, u32[]{:S(2)}, u32[]{:S(2)}) async-start(bf16[8,4,64,256]{3,2,1,0:T(8,128)(2,1)} %first_pass.2.refs_0_), calls=%async_computation.1 | async-start | bytes 2097152 | tf_op jit(solution)/shard_map/all_to_all | solution.py:293
  67.1 1.3 %copy-start = (bf16[8,4,64,256]{3,2,1,0:T(8,128)(2,1)S(1)}, bf16[8,4,64,256]{3,2,1,0:T(8,128)(2,1)}, u32[]{:S(2)}) copy-start(bf16[8,4,64,256]{3,2,1,0:T(8,128)(2,1)} %first_pass.2.refs_0_) | copy-start | bytes 3145732
  68.4 1.0 copy-start.2
  69.4 1.0 copy-start.4
  76.1 9.1 %copy-start.5 = (f32[2,3]{1,0:T(2,128)S(1)}, f32[2,3]{1,0:T(2,128)}, u32[]{:S(2)}) copy-start(f32[2,3]{1,0:T(2,128)} %coef_ref.3) | copy-start | bytes 76
  81.6 21.8 %all-to-all-start.2 = ((bf16[8,4,64,256]{3,2,1,0:T(8,128)(2,1)}), bf16[8,4,64,256]{3,2,1,0:T(8,128)(2,1)S(1)}, u32[]{:S(2)}, u32[]{:S(2)}) async-start(bf16[8,4,64,256]{3,2,1,0:T(8,128)(2,1)} %gate.3), calls=%async_computation.2 | async-start | bytes 2097152 | tf_op jit(solution)/shard_map/all_to_all | solution.py:294
  89.3 22.7 %copy-start.6 = (s32[8,2]{0,1:T(2,128)S(1)}, s32[8,2]{0,1:T(2,128)}, u32[]{:S(2)}) copy-start(s32[8,2]{0,1:T(2,128)} %param.11) | copy-start | bytes 196
  89.3 12.4 %collective-permute-start = (bf16[16,1024]{1,0:T(8,128)(2,1)S(1)}, bf16[16,1024]{1,0:T(8,128)(2,1)S(1)}, u32[]{:S(2)}, u32[]{:S(2)}) collective-permute-start(bf16[16,1024]{1,0:T(8,128)(2,1)S(1)} %get-tuple-element.12), channel_id=1, source_target_pairs={{0,9},{1,10},{2,11},{3,12},{4,13},{5,14},{6,15},{7,0},{8,1},{9,2},... | collective-permute-start | bytes 98312 | tf_op jit(solution)/shard_map/ppermute | solution.py:289
  91.9 9.8 %collective-permute-start.1 = (bf16[16,1024]{1,0:T(8,128)(2,1)S(1)}, bf16[16,1024]{1,0:T(8,128)(2,1)S(1)}, u32[]{:S(2)}, u32[]{:S(2)}) collective-permute-start(bf16[16,1024]{1,0:T(8,128)(2,1)S(1)} %get-tuple-element.13), channel_id=1, source_target_pairs={{0,7},{1,8},{2,9},{3,10},{4,11},{5,12},{6,13},{7,14},{8,15},{9,0},... | collective-permute-start | bytes 98312 | tf_op jit(solution)/shard_map/ppermute | solution.py:289
  101.7 13.6 %collective-permute-start.2 = (bf16[64,2048]{1,0:T(8,128)(2,1)S(1)}, bf16[64,2048]{1,0:T(8,128)(2,1)S(1)}, u32[]{:S(2)}, u32[]{:S(2)}) collective-permute-start(bf16[64,2048]{1,0:T(8,128)(2,1)S(1)} %gate.2.refs_0_), channel_id=1, source_target_pairs={{0,8},{1,9},{2,10},{3,11},{4,12},{5,13},{6,14},{7,15},{8,0},{9,1},... | collective-permute-start | bytes 786440 | tf_op jit(solution)/shard_map/ppermute | solution.py:289
  107.4 7.9 %collective-permute-start.3 = (f32[16,1024]{1,0:T(8,128)S(1)}, f32[16,1024]{1,0:T(8,128)S(1)}, u32[]{:S(2)}, u32[]{:S(2)}) collective-permute-start(f32[16,1024]{1,0:T(8,128)S(1)} %get-tuple-element.15), channel_id=1, source_target_pairs={{0,1},{1,2},{2,3},{3,4},{4,5},{5,6},{6,7},{7,8},{8,9},{9,10},{10,1... | collective-permute-start | bytes 196616 | tf_op jit(solution)/shard_map/ppermute | solution.py:289
  107.5 7.8 %collective-permute-start.4 = (f32[16,1024]{1,0:T(8,128)S(1)}, f32[16,1024]{1,0:T(8,128)S(1)}, u32[]{:S(2)}, u32[]{:S(2)}) collective-permute-start(f32[16,1024]{1,0:T(8,128)S(1)} %get-tuple-element.16), channel_id=1, source_target_pairs={{0,15},{1,0},{2,1},{3,2},{4,3},{5,4},{6,5},{7,6},{8,7},{9,8},{10,9... | collective-permute-start | bytes 196616 | tf_op jit(solution)/shard_map/ppermute | solution.py:289

commit v4 on v3

--- a/solution.py
+++ b/solution.py
@@ -266,7 +266,7 @@
     place = jnp.stack([seg, member == 0, member == groups - 1, index == 0, index == devices - 1]).astype(jnp.int32)
 
     bins = np.arange(slow)
-    tile = min(256, groups * rows)
+    tile = min(128, groups * rows)
     short = np.stack(dft_table(bins, bins, slow)).astype(BF16).reshape(2, -1, tile, slow)
     short = short.transpose(1, 0, 2, 3).reshape(-1, 2 * tile, slow)
     fast = np.arange(width // 4)

time: 119 us -> 120 us (level)
  no operation moved by 1% of the time
where the time goes in v4:
time: 120 us; the launch traced here: 119 us
  waiting for transfers between devices  55.1 us (46%)
  starting transfers between devices  30.1 us (25%)
  Pallas kernels  26.5 us (22%)
  local copies, waits for them, and re-layouts  4.55 us (4%)
  other arithmetic  2.85 us (2%)
    all_to_all x1, waiting for transfers between devices, local(): pieces = trade(pack(series, groups))  37.2 us
    ppermute x5, waiting for transfers between devices, move(): lax.ppermute(x, 'tm', [(i, (i + by) % devices) for i in range(devices)])  13 us
    pallas_call x2, Pallas kernels, first_pass(): pl.pallas_call(first_kernel, grid_spec=pltpu.PrefetchScalarGridSpec(num_s...  12.4 us
    all_to_all x1, starting transfers between devices, local(): far = trade(far, axis_index_groups=halves)  10.3 us
    ppermute x5, starting transfers between devices, move(): lax.ppermute(x, 'tm', [(i, (i + by) % devices) for i in range(devices)])  8.88 us
    pallas_call x2, Pallas kernels, fstat_pass(): pl.pallas_call(functools.partial(fstat_kernel, length), grid=(table.shape...  8.05 us
    all_to_all x1, starting transfers between devices, local(): pieces = trade(pack(series, groups))  7.39 us
    all_to_all x1, waiting for transfers between devices, local(): far = trade(far, axis_index_groups=halves)  4.92 us
  transfers between devices with their start and end apart: 8, of which 4 were waited for; matrix products, arithmetic and copies ran while one was open for 3% of the time, Pallas kernels for 12%

profile of v4, /device:TPU:0, one launch (start us, length us, event | category | flops | bytes accessed | tf_op | source)
XLA Modules:
  0.0 119.3 jit_solution(5135969283934761929)
XLA Ops:
  0.0 2.6 %pack.1 = bf16[16,4,64,256]{3,2,1,0:T(8,128)(2,1)} custom-call(bf16[2,4,64,2048]{3,2,1,0:T(8,128)(2,1)} %x_ref.1), custom_call_target="tpu_custom_call" | custom-call | bytes 4194304 | tf_op jit(solution)/shard_map/pack/pallas_call | solution.py:53
  2.6 7.4 %all-to-all-start = ((bf16[16,4,64,256]{3,2,1,0:T(8,128)(2,1)}), bf16[16,4,64,256]{3,2,1,0:T(8,128)(2,1)S(1)}, u32[]{:S(2)}, u32[]{:S(2)}) async-start(bf16[16,4,64,256]{3,2,1,0:T(8,128)(2,1)} %pack.1), calls=%async_computation | async-start | bytes 4194304 | tf_op jit(solution)/shard_map/all_to_all | solution.py:283
  10.1 1.0 copy.13
  11.1 2.8 %sine_negate_fusion = (f32[1024,1]{1,0:T(8,128)S(1)}, f32[1024,1]{1,0:T(8,128)S(1)}) fusion(f32[1024,1]{1,0:T(8,128)} %copy.13), kind=kLoop, calls=%fused_computation | loop fusion | flops 2048 | bytes 12288 | tf_op jit(solution)/shard_map/neg | solution.py:279
  13.9 0.0 copy-start.1
  13.9 37.2 %all-to-all-done.x_ref = bf16[16,4,64,256]{3,2,1,0:T(8,128)(2,1)S(1)} async-done(((bf16[16,4,64,256]{3,2,1,0:T(8,128)(2,1)}), bf16[16,4,64,256]{3,2,1,0:T(8,128)(2,1)S(1)}, u32[]{:S(2)}, u32[]{:S(2)}) %all-to-all-start) | async-done | bytes 2097184 | tf_op jit(solution)/shard_map/all_to_all | solution.py:283
  51.1 6.2 %first_pass.2.refs_0_ = bf16[8,4,64,256]{3,2,1,0:T(8,128)(2,1)} custom-call(s32[1]{0:T(128)} %bitcast.5.half_ref, bf16[16,4,64,256]{3,2,1,0:T(8,128)(2,1)S(1)} %all-to-all-done.x_ref, bf16[256,256]{1,0:T(8,128)(2,1)} %constant.63.clone.sort_ref, bf16[8,256,1024]{2,1,0:T(8,128)(2,1)} %constant.64.clone.w_ref, f32[1024,256]{1,0:T(8,128)} %constant.65.clone.br_ref, ...), custom_call_target="tpu_custom_call" | custom-call | flops 2147483648 | bytes 2097152 | tf_op jit(solution)/shard_map/first_pass/pallas_call | solution.py:98
  57.3 0.0 copy-done.1
  57.3 10.3 %all-to-all-start.1 = ((bf16[8,4,64,256]{3,2,1,0:T(8,128)(2,1)}), bf16[8,4,64,256]{3,2,1,0:T(8,128)(2,1)S(1)}, u32[]{:S(2)}, u32[]{:S(2)}) async-start(bf16[8,4,64,256]{3,2,1,0:T(8,128)(2,1)} %first_pass.2.refs_0_), calls=%async_computation.1 | async-start | bytes 2097152 | tf_op jit(solution)/shard_map/all_to_all | solution.py:293
  67.6 1.3 %copy-done = bf16[8,4,64,256]{3,2,1,0:T(8,128)(2,1)S(1)} copy-done((bf16[8,4,64,256]{3,2,1,0:T(8,128)(2,1)S(1)}, bf16[8,4,64,256]{3,2,1,0:T(8,128)(2,1)}, u32[]{:S(2)}) %copy-start) | copy-done | bytes 1048600
  68.9 1.0 copy-done.2
  69.9 1.0 copy-done.4
  71.0 6.2 %first_pass.3.refs_0_ = bf16[8,4,64,256]{3,2,1,0:T(8,128)(2,1)} custom-call(s32[1]{0:T(128)} %bitcast.half_ref, bf16[16,4,64,256]{3,2,1,0:T(8,128)(2,1)S(1)} %all-to-all-done.x_ref, bf16[256,256]{1,0:T(8,128)(2,1)} %constant.63.clone.sort_ref, bf16[8,256,1024]{2,1,0:T(8,128)(2,1)} %constant.64.clone.w_ref, f32[1024,256]{1,0:T(8,128)} %constant.65.clone.br_ref, ...), custom_call_target="tpu_custom_call" | custom-call | flops 2147483648 | bytes 2097152 | tf_op jit(solution)/shard_map/first_pass/pallas_call | solution.py:98
  77.2 4.9 %all-to-all-done.1.z_ref.refs_1_ = bf16[8,4,64,256]{3,2,1,0:T(8,128)(2,1)S(1)} async-done(((bf16[8,4,64,256]{3,2,1,0:T(8,128)(2,1)}), bf16[8,4,64,256]{3,2,1,0:T(8,128)(2,1)S(1)}, u32[]{:S(2)}, u32[]{:S(2)}) %all-to-all-start.1) | async-done | bytes 1048608 | tf_op jit(solution)/shard_map/all_to_all | solution.py:293
  82.1 3.6 %all-to-all-start.2 = ((bf16[8,4,64,256]{3,2,1,0:T(8,128)(2,1)}), bf16[8,4,64,256]{3,2,1,0:T(8,128)(2,1)S(1)}, u32[]{:S(2)}, u32[]{:S(2)}) async-start(bf16[8,4,64,256]{3,2,1,0:T(8,128)(2,1)} %gate.3), calls=%async_computation.2 | async-start | bytes 2097152 | tf_op jit(solution)/shard_map/all_to_all | solution.py:294
  85.7 0.1 stack.39.place_ref
  85.7 4.0 %fstat_pass.2 = (bf16[64,2048]{1,0:T(8,128)(2,1)S(1)}, bf16[16,1024]{1,0:T(8,128)(2,1)S(1)}, bf16[16,1024]{1,0:T(8,128)(2,1)S(1)}) custom-call(s32[5]{0:T(128)S(1)} %stack.39.place_ref, f32[2,3]{1,0:T(2,128)S(1)} %copy-done.5, bf16[8,4,64,256]{3,2,1,0:T(8,128)(2,1)S(1)} %all-to-all-done.1.z_ref.refs_1_, bf16[2,4,2,512,256]{4,3,2,1,0:T(8,128)(2,1)} %constant.67.clone.w_ref), custom_call_target="tpu_custom_call" | custom-call | flops 1073741824 | bytes 4194304 | tf_op jit(solution)/shard_map/fstat_pass/pallas_call | solution.py:169
  89.8 0.0 copy-start.6
  89.8 2.6 %collective-permute-start = (bf16[16,1024]{1,0:T(8,128)(2,1)S(1)}, bf16[16,1024]{1,0:T(8,128)(2,1)S(1)}, u32[]{:S(2)}, u32[]{:S(2)}) collective-permute-start(bf16[16,1024]{1,0:T(8,128)(2,1)S(1)} %get-tuple-element.12), channel_id=1, source_target_pairs={{0,9},{1,10},{2,11},{3,12},{4,13},{5,14},{6,15},{7,0},{8,1},{9,2},... | collective-permute-start | bytes 98312 | tf_op jit(solution)/shard_map/ppermute | solution.py:289
  92.4 0.1 collective-permute-start.1
  92.5 9.7 %collective-permute-done.refs_1_.refs_0_ = bf16[16,1024]{1,0:T(8,128)(2,1)S(1)} collective-permute-done((bf16[16,1024]{1,0:T(8,128)(2,1)S(1)}, bf16[16,1024]{1,0:T(8,128)(2,1)S(1)}, u32[]{:S(2)}, u32[]{:S(2)}) %collective-permute-start) | collective-permute-done | bytes 32800 | tf_op jit(solution)/shard_map/ppermute | solution.py:289
  102.2 0.0 collective-permute-done.1.refs_2_.refs_1_
  102.2 1.7 %collective-permute-start.2 = (bf16[64,2048]{1,0:T(8,128)(2,1)S(1)}, bf16[64,2048]{1,0:T(8,128)(2,1)S(1)}, u32[]{:S(2)}, u32[]{:S(2)}) collective-permute-start(bf16[64,2048]{1,0:T(8,128)(2,1)S(1)} %gate.2.refs_0_), channel_id=1, source_target_pairs={{0,8},{1,9},{2,10},{3,11},{4,12},{5,13},{6,14},{7,15},{8,0},{9,1},... | collective-permute-start | bytes 786440 | tf_op jit(solution)/shard_map/ppermute | solution.py:289
  103.9 0.0 all-to-all-done.2.z_ref
  103.9 4.0 %fstat_pass.3 = (f32[64,2048]{1,0:T(8,128)S(1)}, f32[16,1024]{1,0:T(8,128)S(1)}, f32[16,1024]{1,0:T(8,128)S(1)}) custom-call(s32[5]{0:T(128)S(1)} %stack.39.place_ref, f32[2,3]{1,0:T(2,128)S(1)} %copy-done.5, bf16[8,4,64,256]{3,2,1,0:T(8,128)(2,1)S(1)} %all-to-all-done.2.z_ref, bf16[2,4,2,512,256]{4,3,2,1,0:T(8,128)(2,1)} %constant.67.clone.w_ref, ...), custom_call_target="tpu_custom_call" | custom-call | flops 1073741824 | bytes 4194304 | tf_op jit(solution)/shard_map/fstat_pass/pallas_call | solution.py:169
  107.9 0.1 collective-permute-start.3
  108.0 4.4 %collective-permute-start.4 = (f32[16,1024]{1,0:T(8,128)S(1)}, f32[16,1024]{1,0:T(8,128)S(1)}, u32[]{:S(2)}, u32[]{:S(2)}) collective-permute-start(f32[16,1024]{1,0:T(8,128)S(1)} %get-tuple-element.16), channel_id=1, source_target_pairs={{0,15},{1,0},{2,1},{3,2},{4,3},{5,4},{6,5},{7,6},{8,7},{9,8},{10,9... | collective-permute-start | bytes 196616 | tf_op jit(solution)/shard_map/ppermute | solution.py:289
  112.4 0.1 copy.14.offsets_ref
  112.5 3.3 %collective-permute-done.2.other_ref = bf16[64,2048]{1,0:T(8,128)(2,1)S(1)} collective-permute-done((bf16[64,2048]{1,0:T(8,128)(2,1)S(1)}, bf16[64,2048]{1,0:T(8,128)(2,1)S(1)}, u32[]{:S(2)}, u32[]{:S(2)}) %collective-permute-start.2) | collective-permute-done | bytes 262176 | tf_op jit(solution)/shard_map/ppermute | solution.py:289
  115.8 0.0 collective-permute-done.3.refs_2_
  115.8 0.0 collective-permute-done.4.refs_3_
  115.8 3.4 %detect.1 = f32[8,64,2048]{2,1,0:T(8,128)} custom-call(s32[8,2]{1,0:T(8,128)S(1)} %copy.14.offsets_ref, s32[5]{0:T(128)S(1)} %stack.39.place_ref, bf16[64,2048]{1,0:T(8,128)(2,1)S(1)} %collective-permute-done.2.other_ref, f32[64,2048]{1,0:T(8,128)S(1)} %get-tuple-element.14.own_ref, bf16[16,1024]{1,0:T(8,128)(2,1)S(1)} %collective-permute-done.refs_1_.refs_0_, ...), custom_call_target="tpu_custom_call" | custom-call | flops 3145728 | bytes 4194304 | tf_op jit(solution)/shard_map/detect/pallas_call | solution.py:244
  (11 shorter events, 0.0 us)
Async XLA Ops:
  2.6 48.5 %all-to-all-start = ((bf16[16,4,64,256]{3,2,1,0:T(8,128)(2,1)}), bf16[16,4,64,256]{3,2,1,0:T(8,128)(2,1)S(1)}, u32[]{:S(2)}, u32[]{:S(2)}) async-start(bf16[16,4,64,256]{3,2,1,0:T(8,128)(2,1)} %pack.1), calls=%async_computation | async-start | bytes 4194304 | tf_op jit(solution)/shard_map/all_to_all | solution.py:283
  13.9 43.4 %copy-start.1 = (f32[1024,1]{1,0:T(8,128)}, f32[1024,1]{1,0:T(8,128)S(1)}, u32[]{:S(2)}) copy-start(f32[1024,1]{1,0:T(8,128)S(1)} %get-tuple-element.17.vi_ref) | copy-start | bytes 12292
  13.9 43.4 %copy-start.3 = (f32[1024,1]{1,0:T(8,128)}, f32[1024,1]{1,0:T(8,128)S(1)}, u32[]{:S(2)}) copy-start(f32[1024,1]{1,0:T(8,128)S(1)} %get-tuple-element.18.vr_ref) | copy-start | bytes 12292
  57.3 24.7 %all-to-all-start.1 = ((bf16[8,4,64,256]{3,2,1,0:T(8,128)(2,1)}), bf16[8,4,64,256]{3,2,1,0:T(8,128)(2,1)S(1)}, u32[]{:S(2)}, u32[]{:S(2)}) async-start(bf16[8,4,64,256]{3,2,1,0:T(8,128)(2,1)} %first_pass.2.refs_0_), calls=%async_computation.1 | async-start | bytes 2097152 | tf_op jit(solution)/shard_map/all_to_all | solution.py:293
  67.6 1.3 %copy-start = (bf16[8,4,64,256]{3,2,1,0:T(8,128)(2,1)S(1)}, bf16[8,4,64,256]{3,2,1,0:T(8,128)(2,1)}, u32[]{:S(2)}) copy-start(bf16[8,4,64,256]{3,2,1,0:T(8,128)(2,1)} %first_pass.2.refs_0_) | copy-start | bytes 3145732
  68.9 1.0 copy-start.2
  69.9 1.0 copy-start.4
  77.2 8.6 %copy-start.5 = (f32[2,3]{1,0:T(2,128)S(1)}, f32[2,3]{1,0:T(2,128)}, u32[]{:S(2)}) copy-start(f32[2,3]{1,0:T(2,128)} %coef_ref.3) | copy-start | bytes 76
  82.1 21.8 %all-to-all-start.2 = ((bf16[8,4,64,256]{3,2,1,0:T(8,128)(2,1)}), bf16[8,4,64,256]{3,2,1,0:T(8,128)(2,1)S(1)}, u32[]{:S(2)}, u32[]{:S(2)}) async-start(bf16[8,4,64,256]{3,2,1,0:T(8,128)(2,1)} %gate.3), calls=%async_computation.2 | async-start | bytes 2097152 | tf_op jit(solution)/shard_map/all_to_all | solution.py:294
  89.8 22.7 %copy-start.6 = (s32[8,2]{0,1:T(2,128)S(1)}, s32[8,2]{0,1:T(2,128)}, u32[]{:S(2)}) copy-start(s32[8,2]{0,1:T(2,128)} %param.11) | copy-start | bytes 196
  89.8 12.4 %collective-permute-start = (bf16[16,1024]{1,0:T(8,128)(2,1)S(1)}, bf16[16,1024]{1,0:T(8,128)(2,1)S(1)}, u32[]{:S(2)}, u32[]{:S(2)}) collective-permute-start(bf16[16,1024]{1,0:T(8,128)(2,1)S(1)} %get-tuple-element.12), channel_id=1, source_target_pairs={{0,9},{1,10},{2,11},{3,12},{4,13},{5,14},{6,15},{7,0},{8,1},{9,2},... | collective-permute-start | bytes 98312 | tf_op jit(solution)/shard_map/ppermute | solution.py:289
  92.4 9.8 %collective-permute-start.1 = (bf16[16,1024]{1,0:T(8,128)(2,1)S(1)}, bf16[16,1024]{1,0:T(8,128)(2,1)S(1)}, u32[]{:S(2)}, u32[]{:S(2)}) collective-permute-start(bf16[16,1024]{1,0:T(8,128)(2,1)S(1)} %get-tuple-element.13), channel_id=1, source_target_pairs={{0,7},{1,8},{2,9},{3,10},{4,11},{5,12},{6,13},{7,14},{8,15},{9,0},... | collective-permute-start | bytes 98312 | tf_op jit(solution)/shard_map/ppermute | solution.py:289
  102.2 13.6 %collective-permute-start.2 = (bf16[64,2048]{1,0:T(8,128)(2,1)S(1)}, bf16[64,2048]{1,0:T(8,128)(2,1)S(1)}, u32[]{:S(2)}, u32[]{:S(2)}) collective-permute-start(bf16[64,2048]{1,0:T(8,128)(2,1)S(1)} %gate.2.refs_0_), channel_id=1, source_target_pairs={{0,8},{1,9},{2,10},{3,11},{4,12},{5,13},{6,14},{7,15},{8,0},{9,1},... | collective-permute-start | bytes 786440 | tf_op jit(solution)/shard_map/ppermute | solution.py:289
  107.9 7.9 %collective-permute-start.3 = (f32[16,1024]{1,0:T(8,128)S(1)}, f32[16,1024]{1,0:T(8,128)S(1)}, u32[]{:S(2)}, u32[]{:S(2)}) collective-permute-start(f32[16,1024]{1,0:T(8,128)S(1)} %get-tuple-element.15), channel_id=1, source_target_pairs={{0,1},{1,2},{2,3},{3,4},{4,5},{5,6},{6,7},{7,8},{8,9},{9,10},{10,1... | collective-permute-start | bytes 196616 | tf_op jit(solution)/shard_map/ppermute | solution.py:289
  108.0 7.8 %collective-permute-start.4 = (f32[16,1024]{1,0:T(8,128)S(1)}, f32[16,1024]{1,0:T(8,128)S(1)}, u32[]{:S(2)}, u32[]{:S(2)}) collective-permute-start(f32[16,1024]{1,0:T(8,128)S(1)} %get-tuple-element.16), channel_id=1, source_target_pairs={{0,15},{1,0},{2,1},{3,2},{4,3},{5,4},{6,5},{7,6},{8,7},{9,8},{10,9... | collective-permute-start | bytes 196616 | tf_op jit(solution)/shard_map/ppermute | solution.py:289
